TPU v7x, 32 devices: a whole 2x2x4 slice. The times are simulated.
32 devices in a mesh: dp: 2 (over y), table: 16 (over z, x, core).
Axes of the slice: x: 2, y: 2, z: 4, core: 2. Of those that a mesh axis runs over, the one named last changes fastest.
Arguments:
- emb: bfloat16 [256, 256, 192], P(('dp', 'table')), may hold values from -6 to 6
- grad_fm: bfloat16 [256, 6144], P(('dp', 'table')), may hold values from -1.1953125 to 1.1953125
- grad_comp: bfloat16 [256, 256, 192], P(('dp', 'table')), may hold values from -6 to 6
- proj: bfloat16 [256, 24], replicated, may hold values from -0.375 to 0.375
- comp: bfloat16 [256, 256], replicated, may hold values from -0.375 to 0.375
- slot: int32 [256, 256], P(('dp', 'table')), may hold values from 0 to 127, as said below
- counts: int32 [2, 256], P('dp', 'table'), may hold values from 2 to 4, as said below
Outputs:
- row_grads: bfloat16 [2, 256, 128, 192], P('dp', 'table')
- grad_proj: float32 [256, 24], P('table')
- grad_comp: float32 [256, 256], P('table')
Inputs may be any that keep to these rules, and one draw needn't show every extreme that they name: For every group g and table j some sample of g has slot[s, j] = 32 * counts[g, j] - 1, and some has slot[s, j] = 127; entries at or above 32 * counts[g, j] are padded lookups. `counts`: table 0 uses all 4 blocks in every group.
All inputs are finite; a program needn't handle non-finite values.
Results may differ from a plain program's by a relative error of at most 0.0044.
Values may be sent and summed in bfloat16 or wider, within the bound.
No kernel may reach another device: no remote copies, remote signals or barrier semaphores. Data moves between devices by JAX's collectives and lax.ppermute only.
A program may use at most 64 MiB of HBM per device.

v0:
```python
import math

import jax
import jax.numpy as jnp
from jax import lax
from jax.sharding import PartitionSpec as P

BLOCKS = 4


FULL_ACCURACY = lax.Precision.HIGHEST


def input_grads(emb, grad_fm, grad_comp, proj, comp):
    count, width, depth = emb.shape
    rank = proj.shape[1]
    factor_machine_rows = grad_fm.reshape(count, width, rank)
    lower_limit = jnp.einsum("zu,hzy->huy", proj, emb, preferred_element_type=jnp.float32)
    cross_term = jnp.einsum(
        "cuh,cuy->chy", factor_machine_rows, emb, preferred_element_type=jnp.float32
    )
    gradient_list = jnp.einsum(
        "qgs,qsm->qgm",
        factor_machine_rows.astype(jnp.float32),
        lower_limit,
        precision=FULL_ACCURACY,
    )
    gradient_list = gradient_list + jnp.einsum(
        "zs,vsq->vzq", proj.astype(jnp.float32), cross_term, precision=FULL_ACCURACY
    )
    gradient_list = gradient_list + jnp.einsum(
        "cn,bcd->bnd", comp, grad_comp, preferred_element_type=jnp.float32
    )
    return (gradient_list.astype(jnp.bfloat16), cross_term)


def shards(emb, grad_fm, grad_comp, proj, comp, slot, counts):
    count, width, depth = emb.shape
    tables = lax.axis_size("table")
    groups = lax.axis_size("dp")
    local_tables = width // tables
    slot_count = count * tables
    block_rows = slot_count // BLOCKS
    input_grad, cross_term = input_grads(emb, grad_fm, grad_comp, proj, comp)
    rows = input_grad.shape[0]
    sent_values = input_grad.reshape(rows, tables, local_tables, depth)
    sent_slots = slot.reshape(rows, tables, local_tables)
    values = lax.all_to_all(sent_values, "table", split_axis=1, concat_axis=0, tiled=True)
    slots = lax.all_to_all(sent_slots, "table", split_axis=1, concat_axis=0, tiled=True)
    lookups = slots[:, 0, :]
    targets = jnp.arange(slot_count, dtype=jnp.int32)
    onehot = (jnp.transpose(lookups)[:, None, :] == targets[None, :, None]).astype(jnp.bfloat16)
    totals = jnp.einsum("tsl,ltd->tsd", onehot, values[:, 0], preferred_element_type=jnp.float32)
    scale = 1.0 / math.sqrt(count * tables * groups * depth)
    part_proj = (
        jnp.einsum(
            "rvj,ryj->vy",
            emb,
            cross_term,
            precision=FULL_ACCURACY,
            preferred_element_type=jnp.float32,
        )
        * scale
    )
    part_comp = (
        jnp.einsum("bcd,bnd->cn", grad_comp, emb, preferred_element_type=jnp.float32) * scale
    )
    total_proj, total_comp = lax.psum((part_proj, part_comp), ("dp", "table"))
    index = lax.axis_index("table")
    proj_rows = width // tables
    comp_rows = part_comp.shape[0] // tables
    grad_proj = lax.dynamic_slice_in_dim(total_proj, index * proj_rows, proj_rows, 0)
    grad_comp_out = lax.dynamic_slice_in_dim(total_comp, index * comp_rows, comp_rows, 0)
    limits = counts[0] * block_rows
    live = jnp.arange(slot_count, dtype=jnp.int32)[None, :] < limits[:, None]
    rows = jnp.where(live[:, :, None], totals, jnp.float32(0.0)).astype(jnp.bfloat16)[None]
    return (rows, grad_proj, grad_comp_out)


def solution(mesh):
    placed = (
        P(("dp", "table"), None, None),
        P(("dp", "table"), None),
        P(("dp", "table"), None, None),
        P(),
        P(),
        P(("dp", "table"), None),
        P("dp", "table"),
    )
    return jax.shard_map(
        shards,
        mesh=mesh,
        in_specs=placed,
        out_specs=(P("dp", "table", None, None), P("table", None), P("table", None)),
        check_vma=False,
    )
```

profile of v0, /device:TPU:0, one launch (start us, length us, event | category | flops | bytes accessed | tf_op | source)
XLA Modules:
  0.0 175.5 jit_solution(4744654789047643916)
XLA Ops:
  7.2 0.0 copy-start
  7.2 0.0 copy-start.1
  7.2 0.0 copy-start.5
  7.2 0.9 reshape.45
  8.1 0.7 reshape.52
  8.8 7.4 %all-to-all-start = ((s32[16,1,128]{2,1,0:T(1,128)}), s32[16,1,128]{2,1,0:T(1,128)S(1)}, u32[]{:S(2)}, u32[]{:S(2)}) async-start(s32[16,1,128]{2,1,0:T(1,128)} %reshape.52), calls=%async_computation | async-start | bytes 16384 | tf_op jit(solution)/shard_map/all_to_all | solution.py:49
  16.2 1.7 reshape.46
  17.9 1.5 fusion.13
  19.4 0.0 copy-done.1
  19.4 0.0 copy-done.5
  19.4 0.0 copy-start.2
  19.4 0.3 fusion.10
  19.7 0.9 fusion.8
  20.6 0.0 copy-done.2
  20.6 0.0 copy-start.4
  20.6 0.8 fusion.12
  21.4 0.0 copy-done
  21.4 0.1 copy-done.4
  21.5 0.4 fusion.1
  21.9 0.5 copy.26
  22.4 1.1 copy.27
  23.5 0.0 all-to-all-done
  23.5 6.0 %all-to-all-start.1 = ((bf16[8,16,16,192]{3,2,0,1:T(8,128)(2,1)}), bf16[8,16,16,192]{3,2,0,1:T(8,128)(2,1)S(1)}, u32[]{:S(2)}, u32[]{:S(2)}) async-start(bf16[8,16,16,192]{3,2,0,1:T(8,128)(2,1)} %copy.27), calls=%async_computation.1 | async-start | bytes 2097152 | tf_op jit(solution)/shard_map/all_to_all | solution.py:48
  29.5 0.0 copy-start.3
  29.5 0.0 copy-start.6
  29.5 0.0 all-reduce.2.cloned.1.call-start
  29.6 1.1 fusion.2
  30.7 0.0 all-reduce.2.cloned.1.call-update
  30.7 0.0 copy-done.3
  30.7 0.5 fusion.4
  31.2 45.7 %psum.14 = f32[256,24]{0,1:T(8,128)S(1)} all-reduce(f32[256,24]{0,1:T(8,128)S(1)} %fusion.4), channel_id=1, replica_groups=mesh['dp'=2,'table'=16] {'dp','table'}, use_global_device_ids=true, to_apply=%region_0.0 | all-reduce | flops 6144 | bytes 49152 | tf_op jit(solution)/shard_map/psum | solution.py:68
  76.9 0.1 constant_dynamic-slice_fusion.1
  77.0 0.7 copy.29
  77.7 0.0 copy-done.6
  77.7 0.1 iota_compare_fusion.2
  77.8 0.5 broadcast.27
  78.3 0.7 reduce
  79.0 0.1 reshape.53
  79.1 0.1 copy.23
  79.1 86.7 %all-reduce.2.cloned.1.call-done = f32[256,256]{1,0:T(8,128)} async-done(((f32[256,256]{1,0:T(8,128)}), f32[256,256]{1,0:T(8,128)}) %all-reduce.2.cloned.1.call-update) | async-done | bytes 262160 | tf_op jit(solution)/shard_map/psum | solution.py:68
  165.8 1.3 constant_dynamic-slice_fusion
  167.1 0.0 all-to-all-done.1
  167.2 1.5 fusion
  (3 shorter events, 0.0 us)
Async XLA Ops:
  7.2 14.3 %copy-start = (bf16[8,256,192]{1,2,0:T(8,128)(2,1)S(1)}, bf16[8,256,192]{1,2,0:T(8,128)(2,1)}, u32[]{:S(2)}) copy-start(bf16[8,256,192]{1,2,0:T(8,128)(2,1)} %param.9) | copy-start | bytes 2359300
  7.2 12.2 %copy-start.1 = (bf16[8,256,192]{1,2,0:T(8,128)(2,1)S(1)}, bf16[8,256,192]{1,2,0:T(8,128)(2,1)}, u32[]{:S(2)}) copy-start(bf16[8,256,192]{1,2,0:T(8,128)(2,1)} %param.7) | copy-start | bytes 2359300
  7.2 12.2 %copy-start.5 = (bf16[256,24]{0,1:T(8,128)(2,1)S(1)}, bf16[256,24]{0,1:T(8,128)(2,1)}, u32[]{:S(2)}) copy-start(bf16[256,24]{0,1:T(8,128)(2,1)} %param.10) | copy-start | bytes 36868
  8.8 14.7 %all-to-all-start = ((s32[16,1,128]{2,1,0:T(1,128)}), s32[16,1,128]{2,1,0:T(1,128)S(1)}, u32[]{:S(2)}, u32[]{:S(2)}) async-start(s32[16,1,128]{2,1,0:T(1,128)} %reshape.52), calls=%async_computation | async-start | bytes 16384 | tf_op jit(solution)/shard_map/all_to_all | solution.py:49
  19.4 1.2 copy-start.2
  20.6 0.9 copy-start.4
  23.5 143.6 %all-to-all-start.1 = ((bf16[8,16,16,192]{3,2,0,1:T(8,128)(2,1)}), bf16[8,16,16,192]{3,2,0,1:T(8,128)(2,1)S(1)}, u32[]{:S(2)}, u32[]{:S(2)}) async-start(bf16[8,16,16,192]{3,2,0,1:T(8,128)(2,1)} %copy.27), calls=%async_computation.1 | async-start | bytes 2097152 | tf_op jit(solution)/shard_map/all_to_all | solution.py:48
  29.5 1.2 copy-start.3
  29.5 48.2 %copy-start.6 = (s32[1,16]{1,0:T(1,128)S(1)}, s32[1,16]{1,0:T(1,128)}, u32[]{:S(2)}) copy-start(s32[1,16]{1,0:T(1,128)} %param.13) | copy-start | bytes 196
  29.5 136.3 %all-reduce.2.cloned.1.call-start = ((), (), s32[]{:S(2)}) async-start(), calls=%async_computation.2 | async-start | bytes 524288 | tf_op jit(solution)/shard_map/psum | solution.py:68
Sparse Core Ops, SparseCore 0:
  36.5 129.3 all-reduce.1
where the time goes:
time: 176 us; the launch traced here: 175 us
  waiting for transfers between devices  86.7 us (49%)
  blocking collectives  45.7 us (26%)
  between operations  14.2 us (8%)
  starting transfers between devices  13.4 us (8%)
  local copies, waits for them, and re-layouts  7.75 us (4%)
  matrix products  6.9 us (4%)
    psum x1, waiting for transfers between devices, shards(): total_proj, total_comp = lax.psum((part_proj, part_comp), ('dp', 'table'))  86.7 us
    psum x1, blocking collectives, shards(): total_proj, total_comp = lax.psum((part_proj, part_comp), ('dp', 'table'))  45.7 us
    all_to_all x1, starting transfers between devices, shards(): lax.all_to_all(sent_slots, 'table', split_axis=1, concat_axis=0, tiled=True)  7.36 us
    all_to_all x1, starting transfers between devices, shards(): lax.all_to_all(sent_values, 'table', split_axis=1, concat_axis=0, tiled=T...  6.01 us
  transfers between devices with their start and end apart: 3, of which 1 were waited for; matrix products, arithmetic and copies ran while one was open for 7% of the time, Pallas kernels for 0%

commit v1 on v0

v1 whole, which is shorter than its diff:
```python
import math

import jax
import jax.numpy as jnp
from jax import lax
from jax.experimental import pallas as pl
from jax.experimental.pallas import tpu as pltpu
from jax.sharding import PartitionSpec as P

BLOCKS = 4
F32 = jnp.float32
BF16 = jnp.bfloat16
LANES = 128
HALF = 64


def dot(a, b, ca, cb):
    return lax.dot_general(a, b, (((ca,), (cb,)), ((), ())), preferred_element_type=F32)


def iota(shape, dim):
    return lax.broadcasted_iota(jnp.int32, shape, dim)


def round_up(n, m):
    return -(-n // m) * m


def send_kernel(tables, x_ref, h_ref, g_ref, proj_ref, comp_ref, slot_ref, out_ref, spread, main, rest, both):
    count, depth, width = x_ref.shape
    rank = proj_ref.shape[0]
    local = width // tables
    comp_rows = comp_ref.shape[0] // tables
    per = 16
    span = per * rank

    row, col = iota((rank, LANES), 0), iota((rank, LANES), 1)
    eye = ((col == row) | (col == row + rank)).astype(F32)
    fold = jnp.concatenate([eye] * per, axis=0).astype(BF16)
    place = ((col == row + HALF) | (col == row + HALF + rank)).astype(BF16)
    placed_proj = dot(proj_ref[...], place, 0, 0)
    comp_t = comp_ref[...].astype(F32).T.astype(BF16)
    sub, lane = iota((8, span), 0), iota((8, span), 1)
    masks = [(lane >= rank * (sub + 8 * i)) & (lane < rank * (sub + 8 * i + 1)) for i in range(per // 8)]
    lane_l = iota((depth, LANES), 1)
    first = (lane_l % HALF) < rank

    for a in range(width // per):
        block = g_ref[:, a * span:(a + 1) * span].astype(F32)
        for s in range(count):
            wide = jnp.broadcast_to(block[s:s + 1, :], (8, span))
            spread[s, a * per:(a + 1) * per, :] = jnp.concatenate(
                [jnp.where(m, wide, 0.0) for m in masks], axis=0
            ).astype(BF16)

    for s in range(count):
        factors = (dot(spread[s], fold, 1, 0) + placed_proj).astype(BF16)
        terms = dot(x_ref[s], factors, 1, 0)
        high = terms.astype(BF16).astype(F32)
        split = jnp.where(first, high, terms - high)
        both[s * depth:(s + 1) * depth, :] = split.astype(BF16)
        swapped = pltpu.roll(split, HALF, 1).astype(BF16)
        h = h_ref[s]
        h_wide = jnp.concatenate([h, h[LANES:]], axis=0)
        swapped_wide = jnp.concatenate([swapped, swapped[LANES:]], axis=0)
        grads = dot(comp_t, h_wide, 1, 1) + dot(factors, swapped_wide, 1, 1)
        main[pl.ds(s, width, stride=count), :] = grads[:, :LANES]
        rest[pl.ds(s, width, stride=count), :] = grads[:, LANES:]

    x_all = x_ref[...].reshape(count * depth, width)
    h_all = h_ref[...].reshape(count * depth, comp_ref.shape[0])
    comp_grad = dot(h_all, x_all, 0, 0)
    proj_parts = dot(both[...], x_all, 0, 0)
    proj_grad = proj_parts[:rank] + proj_parts[rank:2 * rank]
    slot = slot_ref[...]
    slot_high = slot // 16
    sources = [slot_high.astype(F32), (slot - 16 * slot_high).astype(F32)]
    sources += [proj_grad[8 * i:8 * i + 8] for i in range(rank // 8)]

    rows = local * count
    left = iota((rows // 2, LANES), 1) < HALF
    small = iota((8, LANES), 1)
    tail = out_ref.shape[1] - rows - rows // 2
    for t in range(tables):
        out_ref[t, 0:rows, :] = main[t * rows:(t + 1) * rows, :].astype(BF16)
        upper = rest[t * rows:t * rows + rows // 2, :]
        lower = rest[t * rows + rows // 2:(t + 1) * rows, :]
        out_ref[t, rows:rows + rows // 2, :] = jnp.where(left, upper, lower).astype(BF16)
        part, offset = (t * local) // LANES, (t * local) % LANES
        mixed = jnp.zeros((8, LANES), F32)
        for i, source in enumerate(sources):
            piece = source[:, part * LANES:(part + 1) * LANES]
            shift = (i * local - offset) % LANES
            if shift:
                piece = pltpu.roll(piece, shift, 1)
            mixed = jnp.where((small >= i * local) & (small < (i + 1) * local), piece, mixed)
        mine = comp_grad[t * comp_rows:(t + 1) * comp_rows]
        pieces = [mine[:, i * LANES:(i + 1) * LANES] for i in range(width // LANES)] + [mixed]
        used = comp_rows * (width // LANES) + 8
        if tail > used:
            pieces.append(jnp.zeros((tail - used, LANES), F32))
        out_ref[t, rows + rows // 2:, :] = jnp.concatenate(pieces, axis=0).astype(BF16)


def receive_kernel(block_rows, comp_part, in_ref, counts_ref, rows_ref, sums_ref):
    tables = in_ref.shape[0]
    local, depth, slots = rows_ref.shape
    count = 8
    rows = local * count
    tail = rows + rows // 2
    last = in_ref[:, tail:, :].astype(F32)
    sums_ref[...] = jnp.sum(last, axis=0)
    mixed = last[:, comp_part:comp_part + 8, :]
    slot = 16.0 * mixed[:, :, 0:local] + mixed[:, :, local:2 * local]
    limits = (counts_ref[...] * block_rows).astype(F32)
    slot = jnp.where(slot < limits[None], slot, -1.0)
    target = iota((tables, count, 2 * slots), 2)
    targets = [target.astype(F32), jnp.where(target < slots, -2, target - slots).astype(F32)]
    half_pairs = max(local // 4, 1)
    rest = {}
    for j in range(local // 2):
        hot = jnp.stack(
            [
                (slot[:, :, 2 * j + i:2 * j + i + 1] == targets[i]).astype(F32)
                for i in range(2)
            ],
            axis=1,
        ).reshape(tables * 2 * count, 2 * slots).astype(BF16)
        lead = in_ref[:, 16 * j:16 * j + 16, :].reshape(tables * 16, LANES)
        k = j % half_pairs
        other = in_ref[:, rows + 16 * k:rows + 16 * k + 16, :].reshape(tables * 16, LANES)
        top = dot(lead, hot, 0, 0).astype(BF16)
        bottom = dot(other, hot, 0, 0)
        at = HALF * (j // half_pairs)
        bottom = bottom[at:at + HALF].astype(BF16)
        for i in range(2):
            rows_ref[2 * j + i, 0:LANES, :] = top[:, i * slots:(i + 1) * slots]
            rows_ref[2 * j + i, LANES:, :] = bottom[:, i * slots:(i + 1) * slots]


def finish_kernel(scale, parts, comp_rows, local, rank, *refs):
    ins, (proj_ref, comp_ref) = refs[:parts], refs[parts:]
    total = ins[0][...]
    for ref in ins[1:]:
        total = total + ref[...]
    total = total * scale
    halves = comp_ref.shape[1] // LANES
    comp_ref[...] = jnp.concatenate([total[i * comp_rows:(i + 1) * comp_rows] for i in range(halves)], axis=1)
    mixed = total[halves * comp_rows:halves * comp_rows + 8].T
    proj_ref[...] = jnp.concatenate(
        [mixed[(2 + i) * local:(3 + i) * local, :] for i in range(rank // 8)], axis=1
    )


def shards(emb, grad_fm, grad_comp, proj, comp, slot, counts):
    count, width, depth = emb.shape
    rank = proj.shape[1]
    tables = lax.axis_size("table")
    groups = lax.axis_size("dp")
    local = width // tables
    slot_count = count * tables
    comp_width = comp.shape[0]
    comp_rows = comp_width // tables
    rows = local * count
    comp_part = comp_rows * (width // LANES)
    tail = round_up(comp_part + 8, 16)
    total_rows = rows + rows // 2 + tail
    vmem = pl.BlockSpec(memory_space=pltpu.VMEM)
    params = pltpu.CompilerParams(vmem_limit_bytes=40 * 1024 * 1024)

    def send(*refs):
        send_kernel(tables, *refs)

    sent = pl.pallas_call(
        send,
        out_shape=jax.ShapeDtypeStruct((tables, total_rows, LANES), BF16),
        in_specs=[vmem] * 6,
        out_specs=vmem,
        scratch_shapes=[
            pltpu.VMEM((count, width, 16 * rank), BF16),
            pltpu.VMEM((count * width, LANES), F32),
            pltpu.VMEM((count * width, LANES), F32),
            pltpu.VMEM((count * depth, LANES), BF16),
        ],
        compiler_params=params,
        name="send",
    )(jnp.swapaxes(emb, 1, 2), jnp.swapaxes(grad_comp, 1, 2), grad_fm, proj.T, comp, slot)
    got = lax.all_to_all(sent, "table", split_axis=0, concat_axis=0, tiled=True)

    def receive(*refs):
        receive_kernel(slot_count // BLOCKS, comp_part, *refs)

    row_grads, sums = pl.pallas_call(
        receive,
        out_shape=(
            jax.ShapeDtypeStruct((local, depth, slot_count), BF16),
            jax.ShapeDtypeStruct((tail, LANES), F32),
        ),
        in_specs=[vmem] * 2,
        out_specs=(vmem, vmem),
        compiler_params=params,
        name="receive",
    )(got, counts)
    if groups == 2:
        parts = (sums, lax.ppermute(sums, "dp", [(0, 1), (1, 0)]))
    else:
        parts = (lax.psum(sums, "dp"),)
    scale = 1.0 / math.sqrt(count * tables * groups * depth)

    def finish(*refs):
        finish_kernel(scale, len(parts), comp_rows, local, rank, *refs)

    grad_proj, grad_comp_out = pl.pallas_call(
        finish,
        out_shape=(
            jax.ShapeDtypeStruct((local, rank), F32),
            jax.ShapeDtypeStruct((comp_rows, width), F32),
        ),
        in_specs=[vmem] * len(parts),
        out_specs=(vmem, vmem),
        compiler_params=params,
        name="finish",
    )(*parts)
    return (jnp.swapaxes(row_grads, 1, 2)[None], grad_proj, grad_comp_out)


def solution(mesh):
    placed = (
        P(("dp", "table"), None, None),
        P(("dp", "table"), None),
        P(("dp", "table"), None, None),
        P(),
        P(),
        P(("dp", "table"), None),
        P("dp", "table"),
    )
    return jax.shard_map(
        shards,
        mesh=mesh,
        in_specs=placed,
        out_specs=(P("dp", "table", None, None), P("table", None), P("table", None)),
        check_vma=False,
    )
```

time: 176 us -> 47.8 us (0.27)
  waiting for transfers between devices: 86.7 us -> 2.37 us
  blocking collectives: 45.7 us -> 30.9 us
  between operations: 14.2 us -> 0.66 us
  starting transfers between devices: 13.4 us -> 1.52 us
  matrix products: 6.9 us -> 0 us
  Pallas kernels: 0 us -> 6.51 us
  local copies, waits for them, and re-layouts: 7.75 us -> 5.46 us
    psum x1 -> x0, waiting for transfers between devices: 86.7 us -> none  [shards(): total_proj, total_comp = lax.psum((part_proj, part_comp), ('dp', 'table'))]
    psum x1 -> x0, blocking collectives: 45.7 us -> none  [shards(): total_proj, total_comp = lax.psum((part_proj, part_comp), ('dp', 'table'))]
    all_to_all x0 -> x1, blocking collectives: none -> 30.9 us  [shards(): got = lax.all_to_all(sent, 'table', split_axis=0, concat_axis=0, tiled=True)]
    all_to_all x2 -> x0, starting transfers between devices: 13.4 us -> none  [the longest x1 7.36 us: shards(): lax.all_to_all(sent_slots, 'table', split_axis=1, concat_axis=0, tiled=True)]
    dot_general x8 -> x0, matrix products: 6.9 us -> none  [the longest x1 1.49 us: shards(): jnp.einsum('tsl,ltd->tsd', onehot, values[:, 0], preferred_element_type=j...]
    pallas_call x0 -> x3, Pallas kernels: none -> 6.51 us  [the longest x1 4.02 us: shards(): pl.pallas_call(send, out_shape=jax.ShapeDtypeStruct((tables, total_rows,...]
    unnamed x17 -> x14, local copies, waits for them, and re-layouts: 1.56 us -> 5.46 us
    reshape x4 -> x0, local copies, waits for them, and re-layouts: 3.71 us -> none  [the longest x1 1.71 us: input_grads(): factor_machine_rows = grad_fm.reshape(count, width, rank)]
  transfers between devices with their start and end apart: 3 -> 1, of which waited for: 1 -> 1; matrix products, arithmetic and copies ran while one was open for 7% -> 0% of each run, Pallas kernels for 0% -> 0%
where the time goes in v1:
time: 47.8 us; the launch traced here: 47.4 us
  blocking collectives  30.9 us (65%)
  Pallas kernels  6.51 us (14%)
  local copies, waits for them, and re-layouts  5.46 us (11%)
  waiting for transfers between devices  2.37 us (5%)
  starting transfers between devices  1.52 us (3%)
  between operations  0.66 us (1%)
    all_to_all x1, blocking collectives, shards(): got = lax.all_to_all(sent, 'table', split_axis=0, concat_axis=0, tiled=True)  30.9 us
    unnamed x14, local copies, waits for them, and re-layouts  5.46 us
    pallas_call x1, Pallas kernels, shards(): pl.pallas_call(send, out_shape=jax.ShapeDtypeStruct((tables, total_rows,...  4.02 us
    ppermute x1, waiting for transfers between devices, shards(): parts = (sums, lax.ppermute(sums, 'dp', [(0, 1), (1, 0)]))  2.37 us
    pallas_call x1, Pallas kernels, shards(): pl.pallas_call(receive, out_shape=(jax.ShapeDtypeStruct((local, depth, sl...  1.73 us
    ppermute x1, starting transfers between devices, shards(): parts = (sums, lax.ppermute(sums, 'dp', [(0, 1), (1, 0)]))  1.52 us
  transfers between devices with their start and end apart: 1, of which 1 were waited for; matrix products, arithmetic and copies ran while one was open for 0% of the time, Pallas kernels for 0%

profile of v1, /device:TPU:0, one launch (start us, length us, event | category | flops | bytes accessed | tf_op | source)
XLA Modules:
  0.0 47.4 jit_solution(3039960021656973691)
XLA Ops:
  0.6 0.0 copy-start
  0.6 1.1 %copy-done = bf16[8,256,192]{1,2,0:T(8,128)(2,1)S(1)} copy-done((bf16[8,256,192]{1,2,0:T(8,128)(2,1)S(1)}, bf16[8,256,192]{1,2,0:T(8,128)(2,1)}, u32[]{:S(2)}) %copy-start) | copy-done | bytes 786456
  1.8 0.0 copy-start.1
  1.8 1.1 %copy-done.1 = bf16[8,256,192]{1,2,0:T(8,128)(2,1)S(1)} copy-done((bf16[8,256,192]{1,2,0:T(8,128)(2,1)S(1)}, bf16[8,256,192]{1,2,0:T(8,128)(2,1)}, u32[]{:S(2)}) %copy-start.1) | copy-done | bytes 786456
  2.9 0.0 copy-start.2
  2.9 0.9 %copy-done.2 = bf16[256,256]{1,0:T(8,128)(2,1)S(1)} copy-done((bf16[256,256]{1,0:T(8,128)(2,1)S(1)}, bf16[256,256]{1,0:T(8,128)(2,1)}, u32[]{:S(2)}) %copy-start.2) | copy-done | bytes 131096
  3.8 0.0 copy-start.3
  3.8 0.9 %copy-done.3 = bf16[8,6144]{1,0:T(8,128)(2,1)S(1)} copy-done((bf16[8,6144]{1,0:T(8,128)(2,1)S(1)}, bf16[8,6144]{1,0:T(8,128)(2,1)}, u32[]{:S(2)}) %copy-start.3) | copy-done | bytes 98328
  4.7 0.0 copy-start.4
  4.7 0.7 %copy-done.4 = bf16[256,24]{0,1:T(8,128)(2,1)S(1)} copy-done((bf16[256,24]{0,1:T(8,128)(2,1)S(1)}, bf16[256,24]{0,1:T(8,128)(2,1)}, u32[]{:S(2)}) %copy-start.4) | copy-done | bytes 12312
  5.4 0.0 copy-start.5
  5.4 0.7 %copy-done.5 = s32[8,256]{1,0:T(8,128)S(1)} copy-done((s32[8,256]{1,0:T(8,128)S(1)}, s32[8,256]{1,0:T(8,128)}, u32[]{:S(2)}) %copy-start.5) | copy-done | bytes 8216
  6.1 4.0 %send.1 = bf16[16,240,128]{2,1,0:T(8,128)(2,1)S(1)} custom-call(bf16[8,192,256]{2,1,0:T(8,128)(2,1)S(1)} %bitcast.6, bf16[8,192,256]{2,1,0:T(8,128)(2,1)S(1)} %bitcast.7, bf16[8,6144]{1,0:T(8,128)(2,1)S(1)} %copy-done.3, bf16[24,256]{1,0:T(8,128)(2,1)S(1)} %bitcast.8, bf16[256,256]{1,0:T(8,128)(2,1)S(1)} %copy-done.2, s32[8,256]{1,0:T(8,128)S(1)} %copy-done.5), custom_call_target="tpu_custom_call" | custom-call | tf_op jit(solution)/shard_map/send/pallas_call | solution.py:174
  10.1 0.0 copy-start.6
  10.1 30.9 %all_to_all.5.refs_0_ = bf16[16,240,128]{2,1,0:T(8,128)(2,1)S(1)} all-to-all(bf16[16,240,128]{2,1,0:T(8,128)(2,1)S(1)} %send.1), channel_id=1, replica_groups=mesh['dp'=2,'table'=16] {'table'}, dimensions={0} | all-to-all | bytes 1966080 | tf_op jit(solution)/shard_map/all_to_all | solution.py:188
  41.0 0.0 copy-done.6
  41.0 1.7 %receive.1 = (bf16[16,192,128]{2,1,0:T(8,128)(2,1)}, f32[48,128]{1,0:T(8,128)S(1)}) custom-call(bf16[16,240,128]{2,1,0:T(8,128)(2,1)S(1)} %all_to_all.5.refs_0_, s32[1,16]{1,0:T(1,128)S(1)} %copy-done.6), custom_call_target="tpu_custom_call" | custom-call | tf_op jit(solution)/shard_map/receive/pallas_call | solution.py:193
  42.7 1.5 %collective-permute-start = (f32[48,128]{1,0:T(8,128)S(1)}, f32[48,128]{1,0:T(8,128)S(1)}, u32[]{:S(2)}, u32[]{:S(2)}) collective-permute-start(f32[48,128]{1,0:T(8,128)S(1)} %get-tuple-element.8.refs_0_), channel_id=1, source_target_pairs={{0,16},{16,0},{1,17},{17,1},{2,18},{18,2},{3,19},{19,3},{4,20},{20... | collective-permute-start | bytes 73736 | tf_op jit(solution)/shard_map/ppermute | solution.py:205
  44.3 2.4 %collective-permute-done.refs_1_ = f32[48,128]{1,0:T(8,128)S(1)} collective-permute-done((f32[48,128]{1,0:T(8,128)S(1)}, f32[48,128]{1,0:T(8,128)S(1)}, u32[]{:S(2)}, u32[]{:S(2)}) %collective-permute-start) | collective-permute-done | bytes 24608 | tf_op jit(solution)/shard_map/ppermute | solution.py:205
  46.6 0.8 %finish.1 = (f32[16,24]{1,0:T(8,128)}, f32[16,256]{1,0:T(8,128)}) custom-call(f32[48,128]{1,0:T(8,128)S(1)} %get-tuple-element.8.refs_0_, f32[48,128]{1,0:T(8,128)S(1)} %collective-permute-done.refs_1_), custom_call_target="tpu_custom_call" | custom-call | tf_op jit(solution)/shard_map/finish/pallas_call | solution.py:213
Async XLA Ops:
  0.6 1.1 %copy-start = (bf16[8,256,192]{1,2,0:T(8,128)(2,1)S(1)}, bf16[8,256,192]{1,2,0:T(8,128)(2,1)}, u32[]{:S(2)}) copy-start(bf16[8,256,192]{1,2,0:T(8,128)(2,1)} %param.7) | copy-start | bytes 2359300
  1.8 1.1 %copy-start.1 = (bf16[8,256,192]{1,2,0:T(8,128)(2,1)S(1)}, bf16[8,256,192]{1,2,0:T(8,128)(2,1)}, u32[]{:S(2)}) copy-start(bf16[8,256,192]{1,2,0:T(8,128)(2,1)} %param.9) | copy-start | bytes 2359300
  2.9 0.9 %copy-start.2 = (bf16[256,256]{1,0:T(8,128)(2,1)S(1)}, bf16[256,256]{1,0:T(8,128)(2,1)}, u32[]{:S(2)}) copy-start(bf16[256,256]{1,0:T(8,128)(2,1)} %refs_4_.1) | copy-start | bytes 393220
  3.8 0.9 %copy-start.3 = (bf16[8,6144]{1,0:T(8,128)(2,1)S(1)}, bf16[8,6144]{1,0:T(8,128)(2,1)}, u32[]{:S(2)}) copy-start(bf16[8,6144]{1,0:T(8,128)(2,1)} %refs_2_.1) | copy-start | bytes 294916
  4.7 0.7 %copy-start.4 = (bf16[256,24]{0,1:T(8,128)(2,1)S(1)}, bf16[256,24]{0,1:T(8,128)(2,1)}, u32[]{:S(2)}) copy-start(bf16[256,24]{0,1:T(8,128)(2,1)} %param.10) | copy-start | bytes 36868
  5.4 0.7 %copy-start.5 = (s32[8,256]{1,0:T(8,128)S(1)}, s32[8,256]{1,0:T(8,128)}, u32[]{:S(2)}) copy-start(s32[8,256]{1,0:T(8,128)} %refs_5_.1) | copy-start | bytes 24580
  10.1 30.9 %copy-start.6 = (s32[1,16]{1,0:T(1,128)S(1)}, s32[1,16]{1,0:T(1,128)}, u32[]{:S(2)}) copy-start(s32[1,16]{1,0:T(1,128)} %refs_1_.1) | copy-start | bytes 196
  42.7 3.9 %collective-permute-start = (f32[48,128]{1,0:T(8,128)S(1)}, f32[48,128]{1,0:T(8,128)S(1)}, u32[]{:S(2)}, u32[]{:S(2)}) collective-permute-start(f32[48,128]{1,0:T(8,128)S(1)} %get-tuple-element.8.refs_0_), channel_id=1, source_target_pairs={{0,16},{16,0},{1,17},{17,1},{2,18},{18,2},{3,19},{19,3},{4,20},{20... | collective-permute-start | bytes 73736 | tf_op jit(solution)/shard_map/ppermute | solution.py:205

commit v2 on v1

v2 whole, which is shorter than its diff:
```python
import math

import jax
import jax.numpy as jnp
from jax import lax
from jax.experimental import pallas as pl
from jax.experimental.pallas import tpu as pltpu
from jax.sharding import PartitionSpec as P

BLOCKS = 4
F32 = jnp.float32
BF16 = jnp.bfloat16
LANES = 128
HALF = 64
CROSS = 0
LAST = BF16
STAGES = lambda bits: [[b] for b in range(1, bits - 2)] + [[bits - 2, bits - 1]]


def dot(a, b, ca, cb):
    return lax.dot_general(a, b, (((ca,), (cb,)), ((), ())), preferred_element_type=F32)


def iota(shape, dim):
    return lax.broadcasted_iota(jnp.int32, shape, dim)


def round_up(n, m):
    return -(-n // m) * m


def send_kernel(tables, index_ref, x_hbm, h_hbm, g_hbm, proj_hbm, comp_hbm, slot_hbm, out_hbm, keep_hbm, give_hbm,
                x_ref, h_ref, g_ref, proj_ref, comp_ref, slot_ref, spread, factors, both, swapped, main, rest, out_ref, keep_ref, give_ref, sems):
    count, depth, width = x_ref.shape
    rank = proj_ref.shape[0]
    comp_width = comp_ref.shape[0]
    local, comp_rows = width // tables, comp_width // tables
    block = 8 * rank
    window = 2 * LANES

    pairs = [(g_hbm, g_ref), (proj_hbm, proj_ref), (x_hbm, x_ref), (h_hbm, h_ref), (comp_hbm, comp_ref), (slot_hbm, slot_ref)]
    copies = [pltpu.make_async_copy(a, b, sems.at[i]) for i, (a, b) in enumerate(pairs)]
    for copy in copies:
        copy.start()
    sends = [pltpu.make_async_copy(out_ref.at[t], out_hbm.at[t], sems.at[8 + t]) for t in range(tables)]
    keep_copy = pltpu.make_async_copy(keep_ref, keep_hbm, sems.at[6])
    give_copy = pltpu.make_async_copy(give_ref, give_hbm, sems.at[7])

    row, col = iota((rank, LANES), 0), iota((rank, LANES), 1)
    eye = ((col == row) | (col == row + rank)).astype(F32)
    place = ((col == row + HALF) | (col == row + HALF + rank)).astype(BF16)
    sub, lane = iota((8, window), 0), iota((8, window), 1)
    folds, masks = [], []
    for start in (0, HALF):
        parts = [eye] * 8
        if start:
            parts = [jnp.zeros((start, LANES), F32)] + parts
        if window > start + block:
            parts = parts + [jnp.zeros((window - start - block, LANES), F32)]
        folds.append(jnp.concatenate(parts, axis=0).astype(BF16))
        masks.append((lane >= start + rank * sub) & (lane < start + rank * (sub + 1)))
    first = (iota((depth, LANES), 1) % HALF) < rank

    copies[0].wait()
    copies[1].wait()
    for a in range(width // 8):
        start, odd = (a * block) // LANES * LANES, a % 2
        piece = g_ref[:, start:start + window].astype(F32)
        for s in range(count):
            wide = jnp.broadcast_to(piece[s:s + 1, :], (8, window))
            spread[odd, s * (width // 2) + (a // 2) * 8:s * (width // 2) + (a // 2) * 8 + 8, :] = jnp.where(masks[odd], wide, 0.0).astype(BF16)
    placed_proj = dot(proj_ref[...], place, 0, 0)
    for s in range(count):
        lo, hi = s * (width // 2), (s + 1) * (width // 2)
        halves = [dot(spread[i, lo:hi, :], folds[i], 1, 0).reshape(width // 16, 8, LANES) for i in range(2)]
        columns = jnp.stack(halves, axis=1).reshape(width, LANES)
        factors[s] = (columns + placed_proj).astype(BF16)
    copies[2].wait()
    for s in range(count):
        terms = dot(x_ref[s], factors[s], 1, 0)
        high = terms.astype(BF16).astype(F32)
        split = jnp.where(first, high, terms - high)
        both[s * depth:(s + 1) * depth, :] = split.astype(BF16)
        swapped[s] = pltpu.roll(split, HALF, 1).astype(BF16)
    copies[3].wait()
    copies[4].wait()
    copies[5].wait()

    x_all = x_ref[...].reshape(count * depth, width)
    h_all = h_ref[...].reshape(count * depth, comp_width)
    comp_grad = dot(h_all, x_all, 0, 0)
    proj_parts = dot(both[...], x_all, 0, 0)
    proj_grad = proj_parts[:rank] + proj_parts[rank:2 * rank]
    sources = [proj_grad[8 * i:8 * i + 8] for i in range(rank // 8)]
    even = (index_ref[0] % 2) == 0

    def weight_block(t):
        mine = comp_grad[t * comp_rows:(t + 1) * comp_rows]
        pieces = [mine[:, i * LANES:(i + 1) * LANES] for i in range(width // LANES)]
        return jnp.concatenate(pieces + [gather_lanes(sources, t, local)], axis=0)

    for i in range(tables // 2):
        zero, one = weight_block(2 * i), weight_block(2 * i + 1)
        keep_ref[i] = jnp.where(even, zero, one)
        give_ref[i] = jnp.where(even, one, zero)
    give_copy.start()
    keep_copy.start()

    comp_t = comp_ref[...].astype(F32).T.astype(BF16)
    for s in range(count):
        h, other = h_ref[s], swapped[s]
        h_wide = jnp.concatenate([h, h[LANES:]], axis=0)
        other_wide = jnp.concatenate([other, other[LANES:]], axis=0)
        grads = dot(comp_t, h_wide, 1, 1) + dot(factors[s], other_wide, 1, 1)
        main[pl.ds(s, width, stride=count), :] = grads[:, :LANES]
        rest[pl.ds(s, width, stride=count), :] = grads[:, LANES:]

    slot = slot_ref[...]
    slot_high = slot // 16
    sources = [slot_high.astype(F32), (slot - 16 * slot_high).astype(F32)]
    rows = local * count
    left = iota((rows // 2, LANES), 1) < HALF
    for t in range(tables):
        out_ref[t, 0:rows, :] = main[t * rows:(t + 1) * rows, :].astype(BF16)
        upper = rest[t * rows:t * rows + rows // 2, :]
        lower = rest[t * rows + rows // 2:(t + 1) * rows, :]
        out_ref[t, rows:rows + rows // 2, :] = jnp.where(left, upper, lower).astype(BF16)
        mixed = gather_lanes(sources, t, local)
        out_ref[t, rows + rows // 2:, :] = jnp.concatenate([mixed, mixed], axis=0).astype(BF16)
        sends[t].start()
    give_copy.wait()
    keep_copy.wait()
    for copy in sends:
        copy.wait()


def gather_lanes(sources, t, local):
    part, offset = (t * local) // LANES, (t * local) % LANES
    lane = iota((8, LANES), 1)
    mixed = jnp.zeros((8, LANES), F32)
    for i, source in enumerate(sources):
        piece = source[:, part * LANES:(part + 1) * LANES]
        shift = (i * local - offset) % LANES
        if shift:
            piece = pltpu.roll(piece, shift, 1)
        mixed = jnp.where((lane >= i * local) & (lane < (i + 1) * local), piece, mixed)
    return mixed


def split(blocks, bits, index):
    if not bits:
        return [blocks]
    even = ((index >> bits[0]) % 2) == 0
    keep = [jnp.where(even, zero, one) for zero, one in zip(blocks[0::2], blocks[1::2])]
    give = [jnp.where(even, one, zero) for zero, one in zip(blocks[0::2], blocks[1::2])]
    return [part for pair in zip(split(keep, bits[1:], index), split(give, bits[1:], index)) for part in pair]


def total_of(refs, i):
    parts = [ref[i].astype(F32) for ref in refs]
    while len(parts) > 1:
        parts = [sum(parts[j:j + 2][1:], parts[j]) for j in range(0, len(parts), 2)]
    return parts[0]


def split_kernel(bits, index_ref, *refs):
    ins, outs = refs[:-2 ** len(bits)], refs[-2 ** len(bits):]
    parts = split([total_of(ins, i) for i in range(ins[0].shape[0])], bits, index_ref[0])
    for out, blocks in zip(outs, parts):
        for i, block in enumerate(blocks):
            out[i] = block.astype(out.dtype)


def add_kernel(*refs):
    refs[-1][0] = total_of(refs[:-1], 0)


def finish_kernel(scale, comp_rows, local, rank, after_ref, *refs):
    proj_ref, comp_ref = refs[-2:]
    total = total_of(refs[:-2], 0) * scale
    halves = comp_ref.shape[1] // LANES
    comp_ref[...] = jnp.concatenate([total[i * comp_rows:(i + 1) * comp_rows] for i in range(halves)], axis=1)
    mixed = total[halves * comp_rows:halves * comp_rows + 8].T
    proj_ref[...] = jnp.concatenate([mixed[i * local:(i + 1) * local, :] for i in range(rank // 8)], axis=1)


def hold_kernel(in_ref, out_ref):
    pass


def receive_kernel(block_rows, in_ref, counts_ref, rows_ref, after_ref):
    after_ref[...] = jnp.zeros_like(after_ref)
    tables = in_ref.shape[0]
    local, depth, slots = rows_ref.shape
    count = 8
    rows = local * count
    tail = rows + rows // 2
    mixed = in_ref[:, tail:, :].astype(F32)[:, :8, :]
    slot = 16.0 * mixed[:, :, 0:local] + mixed[:, :, local:2 * local]
    limits = (counts_ref[...] * block_rows).astype(F32)
    slot = jnp.where(slot < limits[None], slot, -1.0)
    target = iota((tables, count, 2 * slots), 2)
    targets = [target.astype(F32), jnp.where(target < slots, -2, target - slots).astype(F32)]
    half_pairs = max(local // 4, 1)
    for j in range(local // 2):
        hot = jnp.stack(
            [(slot[:, :, 2 * j + i:2 * j + i + 1] == targets[i]).astype(F32) for i in range(2)], axis=1
        ).reshape(tables * 2 * count, 2 * slots).astype(BF16)
        lead = in_ref[:, 16 * j:16 * j + 16, :].reshape(tables * 16, LANES)
        k = j % half_pairs
        other = in_ref[:, rows + 16 * k:rows + 16 * k + 16, :].reshape(tables * 16, LANES)
        top = dot(lead, hot, 0, 0).astype(BF16)
        bottom = dot(other, hot, 0, 0)
        at = HALF * (j // half_pairs)
        bottom = bottom[at:at + HALF].astype(BF16)
        for i in range(2):
            rows_ref[2 * j + i, 0:LANES, :] = top[:, i * slots:(i + 1) * slots]
            rows_ref[2 * j + i, LANES:, :] = bottom[:, i * slots:(i + 1) * slots]


def shards(emb, grad_fm, grad_comp, proj, comp, slot, counts):
    count, width, depth = emb.shape
    rank = proj.shape[1]
    tables = lax.axis_size("table")
    groups = lax.axis_size("dp")
    local = width // tables
    slot_count = count * tables
    comp_width = comp.shape[0]
    comp_rows = comp_width // tables
    rows = local * count
    total_rows = rows + rows // 2 + 16
    vmem = pl.BlockSpec(memory_space=pltpu.VMEM)
    smem = pl.BlockSpec(memory_space=pltpu.SMEM)
    hbm = pl.BlockSpec(memory_space=pltpu.HBM)
    params = pltpu.CompilerParams(vmem_limit_bytes=40 * 1024 * 1024)
    large = pltpu.CompilerParams(vmem_limit_bytes=60 * 1024 * 1024)

    def call(body, name, outs, ins, specs, params=params, out=vmem, **more):
        return pl.pallas_call(
            body,
            out_shape=tuple(jax.ShapeDtypeStruct(*o) for o in outs),
            in_specs=specs,
            out_specs=(out,) * len(outs),
            compiler_params=params,
            name=name,
            **more,
        )(*ins)

    x, h = jnp.swapaxes(emb, 1, 2), jnp.swapaxes(grad_comp, 1, 2)
    index = lax.axis_index("table").astype(jnp.int32).reshape(1)
    part = comp_rows * (width // LANES) + 8
    shapes = [((tables, total_rows, LANES), BF16)] + [((tables // 2, part, LANES), F32)] * 2
    sent, keep, give = call(
        lambda *refs: send_kernel(tables, *refs),
        "send",
        shapes,
        (index, x, h, grad_fm, proj.T, comp, slot),
        [smem] + [hbm] * 6,
        params=large,
        out=hbm,
        scratch_shapes=[
            pltpu.VMEM(x.shape, BF16),
            pltpu.VMEM(h.shape, BF16),
            pltpu.VMEM(grad_fm.shape, BF16),
            pltpu.VMEM((rank, width), BF16),
            pltpu.VMEM(comp.shape, BF16),
            pltpu.VMEM(slot.shape, jnp.int32),
            pltpu.VMEM((2, count * width // 2, 2 * LANES), BF16),
            pltpu.VMEM((count, width, LANES), BF16),
            pltpu.VMEM((count * depth, LANES), BF16),
            pltpu.VMEM((count, depth, LANES), BF16),
            pltpu.VMEM((count * width, LANES), F32),
            pltpu.VMEM((count * width, LANES), F32),
        ]
        + [pltpu.VMEM(*o) for o in shapes]
        + [pltpu.SemaphoreType.DMA((8 + tables,))],
    )
    def swap(array, offset, other_group=0):
        pairs = [
            (g * tables + i, (g ^ other_group) * tables + (i ^ offset)) for g in range(groups) for i in range(tables)
        ]
        return lax.ppermute(array, ("dp", "table"), pairs)

    bits = tables.bit_length() - 1
    sums = [keep, swap(give, 1)]
    got = lax.all_to_all(sent, "table", split_axis=0, concat_axis=0, tiled=True)
    for stage in STAGES(bits):
        size = sums[0].shape[0] >> len(stage)
        cross = stage == STAGES(bits)[CROSS] and groups == 2
        kinds = [BF16 if cross else F32] + [BF16 if cross else LAST] * (2 ** len(stage) - 1)
        parts = call(
            lambda *refs, stage=stage: split_kernel(stage, *refs),
            "split",
            [((size, part, LANES), kind) for kind in kinds],
            (index, *sums),
            [smem] + [vmem] * len(sums),
            cost_estimate=pl.CostEstimate(flops=10**11 if stage == STAGES(bits)[0] else 10**6, bytes_accessed=10**6, transcendentals=0),
        )
        sums = [p if o == 0 else swap(p, o << stage[0]) for o, p in enumerate(parts)]
        if cross:
            sums += [swap(p, o << stage[0], 1) for o, p in enumerate(parts)]
    step = 1
    while step < groups and groups != 2:
        keep, = call(add_kernel, "add", [(sums[0].shape, F32)], sums, [vmem] * len(sums))
        sums = [keep, swap(keep, 0, step)]
        step *= 2
    row_grads, after = call(
        lambda *refs: receive_kernel(slot_count // BLOCKS, *refs),
        "receive",
        [((local, depth, slot_count), BF16), ((8, LANES), F32)],
        (got, counts),
        [vmem] * 2,
    )
    scale = 1.0 / math.sqrt(count * tables * groups * depth)
    grad_proj, grad_comp_out = call(
        lambda *refs: finish_kernel(scale, comp_rows, local, rank, *refs),
        "finish",
        [((local, rank), F32), ((comp_rows, width), F32)],
        (after, *sums),
        [vmem] + [vmem] * len(sums),
    )
    return (jnp.swapaxes(row_grads, 1, 2)[None], grad_proj, grad_comp_out)


def solution(mesh):
    placed = (
        P(("dp", "table"), None, None),
        P(("dp", "table"), None),
        P(("dp", "table"), None, None),
        P(),
        P(),
        P(("dp", "table"), None),
        P("dp", "table"),
    )
    return jax.shard_map(
        shards,
        mesh=mesh,
        in_specs=placed,
        out_specs=(P("dp", "table", None, None), P("table", None), P("table", None)),
        check_vma=False,
    )
```

time: 47.8 us -> 36.4 us (0.76)
  blocking collectives: 30.9 us -> 0 us
  starting transfers between devices: 1.52 us -> 15.7 us
  waiting for transfers between devices: 2.37 us -> 13.2 us
  local copies, waits for them, and re-layouts: 5.46 us -> 0.01 us
    all_to_all x1 -> x0, blocking collectives: 30.9 us -> none  [shards(): got = lax.all_to_all(sent, 'table', split_axis=0, concat_axis=0, tiled=True)]
    all_to_all x0 -> x1, starting transfers between devices: none -> 7.15 us  [shards(): got = lax.all_to_all(sent, 'table', split_axis=0, concat_axis=0, tiled=True)]
    ppermute x1 -> x7, starting transfers between devices: 1.52 us -> 8.59 us  [swap(): return lax.ppermute(array, ('dp', 'table'), pairs)]
    ppermute x1 -> x7, waiting for transfers between devices: 2.37 us -> 9.03 us  [swap(): return lax.ppermute(array, ('dp', 'table'), pairs)]
    unnamed x14 -> x4, local copies, waits for them, and re-layouts: 5.46 us -> 0.01 us
    all_to_all x0 -> x1, waiting for transfers between devices: none -> 4.16 us  [shards(): got = lax.all_to_all(sent, 'table', split_axis=0, concat_axis=0, tiled=True)]
    pallas_call x3 -> x5, Pallas kernels: 6.51 us -> 6.55 us  [call(): pl.pallas_call(body, out_shape=tuple((jax.ShapeDtypeStruct(*o) for o in o...]
  transfers between devices with their start and end apart: 1 -> 8, of which waited for: 1 -> 4; matrix products, arithmetic and copies ran while one was open for 0% -> 0% of each run, Pallas kernels for 0% -> 5%
where the time goes in v2:
time: 36.4 us; the launch traced here: 36.2 us
  starting transfers between devices  15.7 us (43%)
  waiting for transfers between devices  13.2 us (36%)
  Pallas kernels  6.55 us (18%)
  between operations  0.7 us (2%)
    ppermute x7, waiting for transfers between devices, swap(): return lax.ppermute(array, ('dp', 'table'), pairs)  9.03 us
    ppermute x7, starting transfers between devices, swap(): return lax.ppermute(array, ('dp', 'table'), pairs)  8.59 us
    all_to_all x1, starting transfers between devices, shards(): got = lax.all_to_all(sent, 'table', split_axis=0, concat_axis=0, tiled=True)  7.15 us
    pallas_call x5, Pallas kernels, call(): pl.pallas_call(body, out_shape=tuple((jax.ShapeDtypeStruct(*o) for o in o...  6.55 us
    all_to_all x1, waiting for transfers between devices, shards(): got = lax.all_to_all(sent, 'table', split_axis=0, concat_axis=0, tiled=True)  4.16 us
  transfers between devices with their start and end apart: 8, of which 4 were waited for; matrix products, arithmetic and copies ran while one was open for 0% of the time, Pallas kernels for 5%

profile of v2, /device:TPU:0, one launch (start us, length us, event | category | flops | bytes accessed | tf_op | source)
XLA Modules:
  0.0 36.2 jit_solution(14555414997310169141)
XLA Ops:
  0.6 4.0 %send.1 = (bf16[16,208,128]{2,1,0:T(8,128)(2,1)}, f32[8,40,128]{2,1,0:T(8,128)}, f32[8,40,128]{2,1,0:T(8,128)}) custom-call(s32[1]{0:T(128)} %bitcast.refs_0_, bf16[8,192,256]{2,1,0:T(8,128)(2,1)} %bitcast.7, bf16[8,192,256]{2,1,0:T(8,128)(2,1)} %bitcast.8, bf16[8,6144]{1,0:T(8,128)(2,1)} %refs_3_.1, bf16[24,256]{1,0:T(8,128)(2,1)} %bitcast.9, ...), custom_call_target="tpu_custom_call" | custom-call | tf_op jit(solution)/shard_map/send/pallas_call | solution.py:239
  4.7 0.5 %collective-permute-start = (f32[8,40,128]{2,1,0:T(8,128)}, f32[8,40,128]{2,1,0:T(8,128)S(1)}, u32[]{:S(2)}, u32[]{:S(2)}) collective-permute-start(f32[8,40,128]{2,1,0:T(8,128)} %get-tuple-element.20), channel_id=1, source_target_pairs={{0,1},{1,0},{2,3},{3,2},{4,5},{5,4},{6,7},{7,6},{8,9},{9,8},{10,11... | collective-permute-start | bytes 491528 | tf_op jit(solution)/shard_map/ppermute | solution.py:282
  5.2 0.0 copy-start.1
  5.2 7.1 %all-to-all-start = ((bf16[16,208,128]{2,1,0:T(8,128)(2,1)}), bf16[16,208,128]{2,1,0:T(8,128)(2,1)S(1)}, u32[]{:S(2)}, u32[]{:S(2)}) async-start(bf16[16,208,128]{2,1,0:T(8,128)(2,1)} %get-tuple-element.16), calls=%async_computation | async-start | bytes 1703936 | tf_op jit(solution)/shard_map/all_to_all | solution.py:286
  12.3 0.0 collective-permute-done.refs_2_
  12.3 0.0 copy-done.1
  12.4 2.0 %collective-permute-start.1 = (bf16[4,40,128]{2,1,0:T(8,128)(2,1)S(1)}, bf16[4,40,128]{2,1,0:T(8,128)(2,1)S(1)}, u32[]{:S(2)}, u32[]{:S(2)}) collective-permute-start(bf16[4,40,128]{2,1,0:T(8,128)(2,1)S(1)} %get-tuple-element.22), channel_id=1, source_target_pairs={{0,2},{1,3},{2,0},{3,1},{4,6},{5,7},{6,4},{7,5},{8,10},{9,11},{10,... | collective-permute-start | bytes 122888 | tf_op jit(solution)/shard_map/ppermute | solution.py:282
  14.4 1.5 %collective-permute-start.2 = (bf16[4,40,128]{2,1,0:T(8,128)(2,1)S(1)}, bf16[4,40,128]{2,1,0:T(8,128)(2,1)S(1)}, u32[]{:S(2)}, u32[]{:S(2)}) collective-permute-start(bf16[4,40,128]{2,1,0:T(8,128)(2,1)S(1)} %get-tuple-element.21.refs_1_), channel_id=1, source_target_pairs={{0,16},{1,17},{2,18},{3,19},{4,20},{5,21},{6,22},{7,23},{8,24},{9,... | collective-permute-start | bytes 122888 | tf_op jit(solution)/shard_map/ppermute | solution.py:282
  15.9 0.1 collective-permute-start.3
  15.9 6.0 %collective-permute-done.1.refs_2_ = bf16[4,40,128]{2,1,0:T(8,128)(2,1)S(1)} collective-permute-done((bf16[4,40,128]{2,1,0:T(8,128)(2,1)S(1)}, bf16[4,40,128]{2,1,0:T(8,128)(2,1)S(1)}, u32[]{:S(2)}, u32[]{:S(2)}) %collective-permute-start.1) | collective-permute-done | bytes 40992 | tf_op jit(solution)/shard_map/ppermute | solution.py:282
  21.9 0.0 collective-permute-done.2.refs_3_
  21.9 1.6 %collective-permute-done.3.refs_4_ = bf16[4,40,128]{2,1,0:T(8,128)(2,1)S(1)} collective-permute-done((bf16[4,40,128]{2,1,0:T(8,128)(2,1)S(1)}, bf16[4,40,128]{2,1,0:T(8,128)(2,1)S(1)}, u32[]{:S(2)}, u32[]{:S(2)}) %collective-permute-start.3) | collective-permute-done | bytes 40992 | tf_op jit(solution)/shard_map/ppermute | solution.py:282
  23.6 0.1 collective-permute-start.4
  23.7 0.0 copy-start
  23.7 4.4 %collective-permute-start.5 = (bf16[1,40,128]{2,1,0:T(8,128)(2,1)S(1)}, bf16[1,40,128]{2,1,0:T(8,128)(2,1)S(1)}, u32[]{:S(2)}, u32[]{:S(2)}) collective-permute-start(bf16[1,40,128]{2,1,0:T(8,128)(2,1)S(1)} %get-tuple-element.25), channel_id=1, source_target_pairs={{0,8},{1,9},{2,10},{3,11},{4,12},{5,13},{6,14},{7,15},{8,0},{9,1},... | collective-permute-start | bytes 30728 | tf_op jit(solution)/shard_map/ppermute | solution.py:282
  28.2 0.0 collective-permute-start.6
  28.2 4.2 %all-to-all-done.refs_0_ = bf16[16,208,128]{2,1,0:T(8,128)(2,1)S(1)} async-done(((bf16[16,208,128]{2,1,0:T(8,128)(2,1)}), bf16[16,208,128]{2,1,0:T(8,128)(2,1)S(1)}, u32[]{:S(2)}, u32[]{:S(2)}) %all-to-all-start) | async-done | bytes 852000 | tf_op jit(solution)/shard_map/all_to_all | solution.py:286
  32.3 0.0 copy-done
  32.3 1.7 %receive.1 = (bf16[16,192,128]{2,1,0:T(8,128)(2,1)}, f32[8,128]{1,0:T(8,128)S(1)}) custom-call(bf16[16,208,128]{2,1,0:T(8,128)(2,1)S(1)} %all-to-all-done.refs_0_, s32[1,16]{1,0:T(1,128)S(1)} %copy-done), custom_call_target="tpu_custom_call" | custom-call | tf_op jit(solution)/shard_map/receive/pallas_call | solution.py:239
  34.0 0.0 collective-permute-done.4.refs_2_
  34.1 1.4 %collective-permute-done.5.refs_3_ = bf16[1,40,128]{2,1,0:T(8,128)(2,1)S(1)} collective-permute-done((bf16[1,40,128]{2,1,0:T(8,128)(2,1)S(1)}, bf16[1,40,128]{2,1,0:T(8,128)(2,1)S(1)}, u32[]{:S(2)}, u32[]{:S(2)}) %collective-permute-start.5) | collective-permute-done | bytes 10272 | tf_op jit(solution)/shard_map/ppermute | solution.py:282
  35.4 0.0 collective-permute-done.6.refs_4_
  35.4 0.8 %finish.1 = (f32[16,24]{1,0:T(8,128)}, f32[16,256]{1,0:T(8,128)}) custom-call(f32[8,128]{1,0:T(8,128)S(1)} %get-tuple-element.18.refs_0_, f32[1,40,128]{2,1,0:T(8,128)S(1)} %get-tuple-element.23.refs_1_, bf16[1,40,128]{2,1,0:T(8,128)(2,1)S(1)} %collective-permute-done.4.refs_2_, bf16[1,40,128]{2,1,0:T(8,128)(2,1)S(1)} %collective-permute-done.5.refs_3_, ...), custom_call_target="tpu_custom_call" | custom-call | tf_op jit(solution)/shard_map/finish/pallas_call | solution.py:239
  (2 shorter events, 0.1 us)
Async XLA Ops:
  4.7 7.7 %collective-permute-start = (f32[8,40,128]{2,1,0:T(8,128)}, f32[8,40,128]{2,1,0:T(8,128)S(1)}, u32[]{:S(2)}, u32[]{:S(2)}) collective-permute-start(f32[8,40,128]{2,1,0:T(8,128)} %get-tuple-element.20), channel_id=1, source_target_pairs={{0,1},{1,0},{2,3},{3,2},{4,5},{5,4},{6,7},{7,6},{8,9},{9,8},{10,11... | collective-permute-start | bytes 491528 | tf_op jit(solution)/shard_map/ppermute | solution.py:282
  5.2 7.2 %copy-start.1 = (f32[8,40,128]{2,1,0:T(8,128)S(1)}, f32[8,40,128]{2,1,0:T(8,128)}, u32[]{:S(2)}) copy-start(f32[8,40,128]{2,1,0:T(8,128)} %get-tuple-element.19.refs_1_) | copy-start | bytes 491524
  5.2 27.1 %all-to-all-start = ((bf16[16,208,128]{2,1,0:T(8,128)(2,1)}), bf16[16,208,128]{2,1,0:T(8,128)(2,1)S(1)}, u32[]{:S(2)}, u32[]{:S(2)}) async-start(bf16[16,208,128]{2,1,0:T(8,128)(2,1)} %get-tuple-element.16), calls=%async_computation | async-start | bytes 1703936 | tf_op jit(solution)/shard_map/all_to_all | solution.py:286
  12.4 9.6 %collective-permute-start.1 = (bf16[4,40,128]{2,1,0:T(8,128)(2,1)S(1)}, bf16[4,40,128]{2,1,0:T(8,128)(2,1)S(1)}, u32[]{:S(2)}, u32[]{:S(2)}) collective-permute-start(bf16[4,40,128]{2,1,0:T(8,128)(2,1)S(1)} %get-tuple-element.22), channel_id=1, source_target_pairs={{0,2},{1,3},{2,0},{3,1},{4,6},{5,7},{6,4},{7,5},{8,10},{9,11},{10,... | collective-permute-start | bytes 122888 | tf_op jit(solution)/shard_map/ppermute | solution.py:282
  14.4 7.6 %collective-permute-start.2 = (bf16[4,40,128]{2,1,0:T(8,128)(2,1)S(1)}, bf16[4,40,128]{2,1,0:T(8,128)(2,1)S(1)}, u32[]{:S(2)}, u32[]{:S(2)}) collective-permute-start(bf16[4,40,128]{2,1,0:T(8,128)(2,1)S(1)} %get-tuple-element.21.refs_1_), channel_id=1, source_target_pairs={{0,16},{1,17},{2,18},{3,19},{4,20},{5,21},{6,22},{7,23},{8,24},{9,... | collective-permute-start | bytes 122888 | tf_op jit(solution)/shard_map/ppermute | solution.py:282
  15.9 7.7 %collective-permute-start.3 = (bf16[4,40,128]{2,1,0:T(8,128)(2,1)S(1)}, bf16[4,40,128]{2,1,0:T(8,128)(2,1)S(1)}, u32[]{:S(2)}, u32[]{:S(2)}) collective-permute-start(bf16[4,40,128]{2,1,0:T(8,128)(2,1)S(1)} %get-tuple-element.22), channel_id=1, source_target_pairs={{0,18},{1,19},{2,16},{3,17},{4,22},{5,23},{6,20},{7,21},{8,26},{9,... | collective-permute-start | bytes 122888 | tf_op jit(solution)/shard_map/ppermute | solution.py:282
  23.6 10.4 %collective-permute-start.4 = (bf16[1,40,128]{2,1,0:T(8,128)(2,1)S(1)}, bf16[1,40,128]{2,1,0:T(8,128)(2,1)S(1)}, u32[]{:S(2)}, u32[]{:S(2)}) collective-permute-start(bf16[1,40,128]{2,1,0:T(8,128)(2,1)S(1)} %get-tuple-element.24), channel_id=1, source_target_pairs={{0,4},{1,5},{2,6},{3,7},{4,0},{5,1},{6,2},{7,3},{8,12},{9,13},{10,... | collective-permute-start | bytes 30728 | tf_op jit(solution)/shard_map/ppermute | solution.py:282
  23.7 8.6 %copy-start = (s32[1,16]{1,0:T(1,128)S(1)}, s32[1,16]{1,0:T(1,128)}, u32[]{:S(2)}) copy-start(s32[1,16]{1,0:T(1,128)} %refs_1_.1) | copy-start | bytes 196
  23.7 11.7 %collective-permute-start.5 = (bf16[1,40,128]{2,1,0:T(8,128)(2,1)S(1)}, bf16[1,40,128]{2,1,0:T(8,128)(2,1)S(1)}, u32[]{:S(2)}, u32[]{:S(2)}) collective-permute-start(bf16[1,40,128]{2,1,0:T(8,128)(2,1)S(1)} %get-tuple-element.25), channel_id=1, source_target_pairs={{0,8},{1,9},{2,10},{3,11},{4,12},{5,13},{6,14},{7,15},{8,0},{9,1},... | collective-permute-start | bytes 30728 | tf_op jit(solution)/shard_map/ppermute | solution.py:282
  28.2 7.3 %collective-permute-start.6 = (bf16[1,40,128]{2,1,0:T(8,128)(2,1)S(1)}, bf16[1,40,128]{2,1,0:T(8,128)(2,1)S(1)}, u32[]{:S(2)}, u32[]{:S(2)}) collective-permute-start(bf16[1,40,128]{2,1,0:T(8,128)(2,1)S(1)} %get-tuple-element.26), channel_id=1, source_target_pairs={{0,12},{1,13},{2,14},{3,15},{4,8},{5,9},{6,10},{7,11},{8,4},{9,5},... | collective-permute-start | bytes 30728 | tf_op jit(solution)/shard_map/ppermute | solution.py:282

commit v3 on v2

--- a/solution.py
+++ b/solution.py
@@ -29,8 +29,8 @@
     return -(-n // m) * m
 
 
-def send_kernel(tables, index_ref, x_hbm, h_hbm, g_hbm, proj_hbm, comp_hbm, slot_hbm, out_hbm, keep_hbm, give_hbm,
-                x_ref, h_ref, g_ref, proj_ref, comp_ref, slot_ref, spread, factors, both, swapped, main, rest, out_ref, keep_ref, give_ref, sems):
+def send_kernel(tables, x_hbm, h_hbm, g_hbm, proj_hbm, comp_hbm, slot_hbm, out_hbm, both_hbm,
+                x_ref, h_ref, g_ref, proj_ref, comp_ref, slot_ref, spread, factors, both, swapped, main, rest, out_ref, sems):
     count, depth, width = x_ref.shape
     rank = proj_ref.shape[0]
     comp_width = comp_ref.shape[0]
@@ -40,11 +40,19 @@
 
     pairs = [(g_hbm, g_ref), (proj_hbm, proj_ref), (x_hbm, x_ref), (h_hbm, h_ref), (comp_hbm, comp_ref), (slot_hbm, slot_ref)]
     copies = [pltpu.make_async_copy(a, b, sems.at[i]) for i, (a, b) in enumerate(pairs)]
-    for copy in copies:
+    pieces = 4
+    for i, (a, b) in enumerate(pairs[2:4]):
+        size = count // pieces
+        copies[2 + i] = [
+            pltpu.make_async_copy(
+                a.at[p * size:(p + 1) * size], b.at[p * size:(p + 1) * size], sems.at[8 + tables + i * pieces + p]
+            )
+            for p in range(pieces)
+        ]
+    for copy in copies[:2] + copies[2] + copies[3] + copies[4:]:
         copy.start()
     sends = [pltpu.make_async_copy(out_ref.at[t], out_hbm.at[t], sems.at[8 + t]) for t in range(tables)]
-    keep_copy = pltpu.make_async_copy(keep_ref, keep_hbm, sems.at[6])
-    give_copy = pltpu.make_async_copy(give_ref, give_hbm, sems.at[7])
+    both_copy = pltpu.make_async_copy(both, both_hbm, sems.at[6])
 
     row, col = iota((rank, LANES), 0), iota((rank, LANES), 1)
     eye = ((col == row) | (col == row + rank)).astype(F32)
@@ -75,36 +83,20 @@
         halves = [dot(spread[i, lo:hi, :], folds[i], 1, 0).reshape(width // 16, 8, LANES) for i in range(2)]
         columns = jnp.stack(halves, axis=1).reshape(width, LANES)
         factors[s] = (columns + placed_proj).astype(BF16)
-    copies[2].wait()
+    for copy in copies[2]:
+        copy.wait()
     for s in range(count):
         terms = dot(x_ref[s], factors[s], 1, 0)
         high = terms.astype(BF16).astype(F32)
         split = jnp.where(first, high, terms - high)
         both[s * depth:(s + 1) * depth, :] = split.astype(BF16)
         swapped[s] = pltpu.roll(split, HALF, 1).astype(BF16)
-    copies[3].wait()
+    for copy in copies[3]:
+        copy.wait()
     copies[4].wait()
     copies[5].wait()
 
-    x_all = x_ref[...].reshape(count * depth, width)
-    h_all = h_ref[...].reshape(count * depth, comp_width)
-    comp_grad = dot(h_all, x_all, 0, 0)
-    proj_parts = dot(both[...], x_all, 0, 0)
-    proj_grad = proj_parts[:rank] + proj_parts[rank:2 * rank]
-    sources = [proj_grad[8 * i:8 * i + 8] for i in range(rank // 8)]
-    even = (index_ref[0] % 2) == 0
-
-    def weight_block(t):
-        mine = comp_grad[t * comp_rows:(t + 1) * comp_rows]
-        pieces = [mine[:, i * LANES:(i + 1) * LANES] for i in range(width // LANES)]
-        return jnp.concatenate(pieces + [gather_lanes(sources, t, local)], axis=0)
-
-    for i in range(tables // 2):
-        zero, one = weight_block(2 * i), weight_block(2 * i + 1)
-        keep_ref[i] = jnp.where(even, zero, one)
-        give_ref[i] = jnp.where(even, one, zero)
-    give_copy.start()
-    keep_copy.start()
+    both_copy.start()
 
     comp_t = comp_ref[...].astype(F32).T.astype(BF16)
     for s in range(count):
@@ -126,11 +118,9 @@
         lower = rest[t * rows + rows // 2:(t + 1) * rows, :]
         out_ref[t, rows:rows + rows // 2, :] = jnp.where(left, upper, lower).astype(BF16)
         mixed = gather_lanes(sources, t, local)
-        out_ref[t, rows + rows // 2:, :] = jnp.concatenate([mixed, mixed], axis=0).astype(BF16)
+        out_ref[t, rows + rows // 2:, :] = mixed.astype(BF16)
         sends[t].start()
-    give_copy.wait()
-    keep_copy.wait()
-    for copy in sends:
+    for copy in [both_copy] + sends:
         copy.wait()
 
 
@@ -147,6 +137,29 @@
     return mixed
 
 
+def weights_kernel(tables, rank, index_ref, x_ref, h_ref, both, keep_ref, give_ref):
+    count, depth, width = x_ref.shape
+    comp_width = h_ref.shape[2]
+    local, comp_rows = width // tables, comp_width // tables
+    x_all = x_ref[...].reshape(count * depth, width)
+    h_all = h_ref[...].reshape(count * depth, comp_width)
+    comp_grad = dot(h_all, x_all, 0, 0)
+    proj_parts = dot(both[...], x_all, 0, 0)
+    proj_grad = proj_parts[:rank] + proj_parts[rank:2 * rank]
+    sources = [proj_grad[8 * i:8 * i + 8] for i in range(rank // 8)]
+    even = (index_ref[0] % 2) == 0
+
+    def weight_block(t):
+        mine = comp_grad[t * comp_rows:(t + 1) * comp_rows]
+        pieces = [mine[:, i * LANES:(i + 1) * LANES] for i in range(width // LANES)]
+        return jnp.concatenate(pieces + [gather_lanes(sources, t, local)], axis=0)
+
+    for i in range(tables // 2):
+        zero, one = weight_block(2 * i), weight_block(2 * i + 1)
+        keep_ref[i] = jnp.where(even, zero, one)
+        give_ref[i] = jnp.where(even, one, zero)
+
+
 def split(blocks, bits, index):
     if not bits:
         return [blocks]
@@ -188,8 +201,9 @@
     pass
 
 
-def receive_kernel(block_rows, in_ref, counts_ref, rows_ref, after_ref):
+def receive_kernel(block_rows, in_ref, counts_ref, rows_hbm, after_ref, rows_ref, sems):
     after_ref[...] = jnp.zeros_like(after_ref)
+    copies = []
     tables = in_ref.shape[0]
     local, depth, slots = rows_ref.shape
     count = 8
@@ -216,6 +230,11 @@
         for i in range(2):
             rows_ref[2 * j + i, 0:LANES, :] = top[:, i * slots:(i + 1) * slots]
             rows_ref[2 * j + i, LANES:, :] = bottom[:, i * slots:(i + 1) * slots]
+        pair = pl.ds(2 * j, 2)
+        copies.append(pltpu.make_async_copy(rows_ref.at[pair], rows_hbm.at[pair], sems.at[j]))
+        copies[j].start()
+    for copy in copies:
+        copy.wait()
 
 
 def shards(emb, grad_fm, grad_comp, proj, comp, slot, counts):
@@ -228,7 +247,7 @@
     comp_width = comp.shape[0]
     comp_rows = comp_width // tables
     rows = local * count
-    total_rows = rows + rows // 2 + 16
+    total_rows = rows + rows // 2 + 8
     vmem = pl.BlockSpec(memory_space=pltpu.VMEM)
     smem = pl.BlockSpec(memory_space=pltpu.SMEM)
     hbm = pl.BlockSpec(memory_space=pltpu.HBM)
@@ -240,7 +259,7 @@
             body,
             out_shape=tuple(jax.ShapeDtypeStruct(*o) for o in outs),
             in_specs=specs,
-            out_specs=(out,) * len(outs),
+            out_specs=out if isinstance(out, tuple) else (out,) * len(outs),
             compiler_params=params,
             name=name,
             **more,
@@ -249,13 +268,13 @@
     x, h = jnp.swapaxes(emb, 1, 2), jnp.swapaxes(grad_comp, 1, 2)
     index = lax.axis_index("table").astype(jnp.int32).reshape(1)
     part = comp_rows * (width // LANES) + 8
-    shapes = [((tables, total_rows, LANES), BF16)] + [((tables // 2, part, LANES), F32)] * 2
-    sent, keep, give = call(
+    shapes = [((tables, total_rows, LANES), BF16), ((count * depth, LANES), BF16)]
+    sent, both = call(
         lambda *refs: send_kernel(tables, *refs),
         "send",
         shapes,
-        (index, x, h, grad_fm, proj.T, comp, slot),
-        [smem] + [hbm] * 6,
+        (x, h, grad_fm, proj.T, comp, slot),
+        [hbm] * 6,
         params=large,
         out=hbm,
         scratch_shapes=[
@@ -272,8 +291,8 @@
             pltpu.VMEM((count * width, LANES), F32),
             pltpu.VMEM((count * width, LANES), F32),
         ]
-        + [pltpu.VMEM(*o) for o in shapes]
-        + [pltpu.SemaphoreType.DMA((8 + tables,))],
+        + [pltpu.VMEM(*shapes[0])]
+        + [pltpu.SemaphoreType.DMA((16 + tables,))],
     )
     def swap(array, offset, other_group=0):
         pairs = [
@@ -282,8 +301,15 @@
         return lax.ppermute(array, ("dp", "table"), pairs)
 
     bits = tables.bit_length() - 1
+    got = lax.all_to_all(sent, "table", split_axis=0, concat_axis=0, tiled=True)
+    keep, give = call(
+        lambda *refs: weights_kernel(tables, rank, *refs),
+        "weights",
+        [((tables // 2, part, LANES), F32)] * 2,
+        (index, x, h, both),
+        [smem] + [vmem] * 3,
+    )
     sums = [keep, swap(give, 1)]
-    got = lax.all_to_all(sent, "table", split_axis=0, concat_axis=0, tiled=True)
     for stage in STAGES(bits):
         size = sums[0].shape[0] >> len(stage)
         cross = stage == STAGES(bits)[CROSS] and groups == 2
@@ -294,7 +320,7 @@
             [((size, part, LANES), kind) for kind in kinds],
             (index, *sums),
             [smem] + [vmem] * len(sums),
-            cost_estimate=pl.CostEstimate(flops=10**11 if stage == STAGES(bits)[0] else 10**6, bytes_accessed=10**6, transcendentals=0),
+            cost_estimate=pl.CostEstimate(flops=10**6, bytes_accessed=10**6, transcendentals=0),
         )
         sums = [p if o == 0 else swap(p, o << stage[0]) for o, p in enumerate(parts)]
         if cross:
@@ -310,6 +336,8 @@
         [((local, depth, slot_count), BF16), ((8, LANES), F32)],
         (got, counts),
         [vmem] * 2,
+        out=(hbm, vmem),
+        scratch_shapes=[pltpu.VMEM((local, depth, slot_count), BF16), pltpu.SemaphoreType.DMA((local // 2,))],
     )
     scale = 1.0 / math.sqrt(count * tables * groups * depth)
     grad_proj, grad_comp_out = call(

time: 36.4 us -> 35.3 us (0.970)
  waiting for transfers between devices: 13.2 us -> 10.5 us
  local copies, waits for them, and re-layouts: 0.01 us -> 1.01 us
  starting transfers between devices: 15.7 us -> 16.1 us
    ppermute x7, waiting for transfers between devices: 9.03 us -> 7.43 us  [swap(): return lax.ppermute(array, ('dp', 'table'), pairs)]
    all_to_all x1, waiting for transfers between devices: 4.16 us -> 3.11 us  [shards(): got = lax.all_to_all(sent, 'table', split_axis=0, concat_axis=0, tiled=True)]
    unnamed x4 -> x8, local copies, waits for them, and re-layouts: 0.01 us -> 1.01 us
    pallas_call x5 -> x6, Pallas kernels: 6.55 us -> 6.61 us  [call(): pl.pallas_call(body, out_shape=tuple((jax.ShapeDtypeStruct(*o) for o in o...]
  transfers between devices with their start and end apart: 8 -> 8, of which waited for: 4 -> 6; matrix products, arithmetic and copies ran while one was open for 0% -> 0% of each run, Pallas kernels for 5% -> 6%
where the time goes in v3:
time: 35.3 us; the launch traced here: 35 us
  starting transfers between devices  16.1 us (46%)
  waiting for transfers between devices  10.5 us (30%)
  Pallas kernels  6.61 us (19%)
  local copies, waits for them, and re-layouts  1.01 us (3%)
  between operations  0.73 us (2%)
    ppermute x7, starting transfers between devices, swap(): return lax.ppermute(array, ('dp', 'table'), pairs)  8.61 us
    all_to_all x1, starting transfers between devices, shards(): got = lax.all_to_all(sent, 'table', split_axis=0, concat_axis=0, tiled=True)  7.49 us
    ppermute x7, waiting for transfers between devices, swap(): return lax.ppermute(array, ('dp', 'table'), pairs)  7.43 us
    pallas_call x6, Pallas kernels, call(): pl.pallas_call(body, out_shape=tuple((jax.ShapeDtypeStruct(*o) for o in o...  6.61 us
    all_to_all x1, waiting for transfers between devices, shards(): got = lax.all_to_all(sent, 'table', split_axis=0, concat_axis=0, tiled=True)  3.11 us
    unnamed x8, local copies, waits for them, and re-layouts  1.01 us
  transfers between devices with their start and end apart: 8, of which 6 were waited for; matrix products, arithmetic and copies ran while one was open for 0% of the time, Pallas kernels for 6%

profile of v3, /device:TPU:0, one launch (start us, length us, event | category | flops | bytes accessed | tf_op | source)
XLA Modules:
  0.0 35.0 jit_solution(14713370388173472675)
XLA Ops:
  0.6 3.7 %send.1 = (bf16[16,200,128]{2,1,0:T(8,128)(2,1)}, bf16[1536,128]{1,0:T(8,128)(2,1)}) custom-call(bf16[8,192,256]{2,1,0:T(8,128)(2,1)} %bitcast.7, bf16[8,192,256]{2,1,0:T(8,128)(2,1)} %bitcast.9, bf16[8,6144]{1,0:T(8,128)(2,1)} %refs_2_.1, bf16[24,256]{1,0:T(8,128)(2,1)} %bitcast.11, bf16[256,256]{1,0:T(8,128)(2,1)} %refs_4_.1, s32[8,256]{1,0:T(8,128)} %refs_5_.1), custom_call_target="tpu_custom_call" | custom-call | tf_op jit(solution)/shard_map/send/pallas_call | solution.py:258
  4.3 0.0 copy-start
  4.3 0.0 copy-start.1
  4.3 7.5 %all-to-all-start = ((bf16[16,200,128]{2,1,0:T(8,128)(2,1)}), bf16[16,200,128]{2,1,0:T(8,128)(2,1)S(1)}, u32[]{:S(2)}, u32[]{:S(2)}) async-start(bf16[16,200,128]{2,1,0:T(8,128)(2,1)} %get-tuple-element.17), calls=%async_computation | async-start | bytes 1638400 | tf_op jit(solution)/shard_map/all_to_all | solution.py:304
  11.8 0.0 copy-done
  11.8 0.0 copy-done.1
  11.9 0.0 copy-start.2
  11.9 1.0 %copy-done.2 = bf16[1536,128]{1,0:T(8,128)(2,1)S(1)} copy-done((bf16[1536,128]{1,0:T(8,128)(2,1)S(1)}, bf16[1536,128]{1,0:T(8,128)(2,1)}, u32[]{:S(2)}) %copy-start.2) | copy-done | bytes 393240
  12.9 0.6 %weights.1 = (f32[8,40,128]{2,1,0:T(8,128)S(1)}, f32[8,40,128]{2,1,0:T(8,128)S(1)}) custom-call(s32[1]{0:T(128)} %bitcast.5.refs_0_, bf16[8,192,256]{2,1,0:T(8,128)(2,1)S(1)} %bitcast.8, bf16[8,192,256]{2,1,0:T(8,128)(2,1)S(1)} %bitcast.10, bf16[1536,128]{1,0:T(8,128)(2,1)S(1)} %copy-done.2), custom_call_target="tpu_custom_call" | custom-call | tf_op jit(solution)/shard_map/weights/pallas_call | solution.py:258
  13.4 0.5 %collective-permute-start = (f32[8,40,128]{2,1,0:T(8,128)S(1)}, f32[8,40,128]{2,1,0:T(8,128)S(1)}, u32[]{:S(2)}, u32[]{:S(2)}) collective-permute-start(f32[8,40,128]{2,1,0:T(8,128)S(1)} %get-tuple-element.22), channel_id=1, source_target_pairs={{0,1},{1,0},{2,3},{3,2},{4,5},{5,4},{6,7},{7,6},{8,9},{9,8},{10,11... | collective-permute-start | bytes 491528 | tf_op jit(solution)/shard_map/ppermute | solution.py:301
  13.9 1.0 %collective-permute-done.refs_2_ = f32[8,40,128]{2,1,0:T(8,128)S(1)} collective-permute-done((f32[8,40,128]{2,1,0:T(8,128)S(1)}, f32[8,40,128]{2,1,0:T(8,128)S(1)}, u32[]{:S(2)}, u32[]{:S(2)}) %collective-permute-start) | collective-permute-done | bytes 163872 | tf_op jit(solution)/shard_map/ppermute | solution.py:301
  15.0 1.9 %collective-permute-start.1 = (bf16[4,40,128]{2,1,0:T(8,128)(2,1)S(1)}, bf16[4,40,128]{2,1,0:T(8,128)(2,1)S(1)}, u32[]{:S(2)}, u32[]{:S(2)}) collective-permute-start(bf16[4,40,128]{2,1,0:T(8,128)(2,1)S(1)} %get-tuple-element.24), channel_id=1, source_target_pairs={{0,2},{1,3},{2,0},{3,1},{4,6},{5,7},{6,4},{7,5},{8,10},{9,11},{10,... | collective-permute-start | bytes 122888 | tf_op jit(solution)/shard_map/ppermute | solution.py:301
  16.9 1.5 %collective-permute-start.2 = (bf16[4,40,128]{2,1,0:T(8,128)(2,1)S(1)}, bf16[4,40,128]{2,1,0:T(8,128)(2,1)S(1)}, u32[]{:S(2)}, u32[]{:S(2)}) collective-permute-start(bf16[4,40,128]{2,1,0:T(8,128)(2,1)S(1)} %get-tuple-element.23.refs_1_), channel_id=1, source_target_pairs={{0,16},{1,17},{2,18},{3,19},{4,20},{5,21},{6,22},{7,23},{8,24},{9,... | collective-permute-start | bytes 122888 | tf_op jit(solution)/shard_map/ppermute | solution.py:301
  18.4 0.1 collective-permute-start.3
  18.5 1.7 %collective-permute-done.1.refs_2_ = bf16[4,40,128]{2,1,0:T(8,128)(2,1)S(1)} collective-permute-done((bf16[4,40,128]{2,1,0:T(8,128)(2,1)S(1)}, bf16[4,40,128]{2,1,0:T(8,128)(2,1)S(1)}, u32[]{:S(2)}, u32[]{:S(2)}) %collective-permute-start.1) | collective-permute-done | bytes 40992 | tf_op jit(solution)/shard_map/ppermute | solution.py:301
  20.2 0.7 %collective-permute-done.2.refs_3_ = bf16[4,40,128]{2,1,0:T(8,128)(2,1)S(1)} collective-permute-done((bf16[4,40,128]{2,1,0:T(8,128)(2,1)S(1)}, bf16[4,40,128]{2,1,0:T(8,128)(2,1)S(1)}, u32[]{:S(2)}, u32[]{:S(2)}) %collective-permute-start.2) | collective-permute-done | bytes 40992 | tf_op jit(solution)/shard_map/ppermute | solution.py:301
  20.9 2.6 %collective-permute-done.3.refs_4_ = bf16[4,40,128]{2,1,0:T(8,128)(2,1)S(1)} collective-permute-done((bf16[4,40,128]{2,1,0:T(8,128)(2,1)S(1)}, bf16[4,40,128]{2,1,0:T(8,128)(2,1)S(1)}, u32[]{:S(2)}, u32[]{:S(2)}) %collective-permute-start.3) | collective-permute-done | bytes 40992 | tf_op jit(solution)/shard_map/ppermute | solution.py:301
  23.5 2.1 %collective-permute-start.4 = (bf16[1,40,128]{2,1,0:T(8,128)(2,1)S(1)}, bf16[1,40,128]{2,1,0:T(8,128)(2,1)S(1)}, u32[]{:S(2)}, u32[]{:S(2)}) collective-permute-start(bf16[1,40,128]{2,1,0:T(8,128)(2,1)S(1)} %get-tuple-element.26), channel_id=1, source_target_pairs={{0,4},{1,5},{2,6},{3,7},{4,0},{5,1},{6,2},{7,3},{8,12},{9,13},{10,... | collective-permute-start | bytes 30728 | tf_op jit(solution)/shard_map/ppermute | solution.py:301
  25.6 0.0 copy-start.3
  25.6 1.9 %collective-permute-start.5 = (bf16[1,40,128]{2,1,0:T(8,128)(2,1)S(1)}, bf16[1,40,128]{2,1,0:T(8,128)(2,1)S(1)}, u32[]{:S(2)}, u32[]{:S(2)}) collective-permute-start(bf16[1,40,128]{2,1,0:T(8,128)(2,1)S(1)} %get-tuple-element.27), channel_id=1, source_target_pairs={{0,8},{1,9},{2,10},{3,11},{4,12},{5,13},{6,14},{7,15},{8,0},{9,1},... | collective-permute-start | bytes 30728 | tf_op jit(solution)/shard_map/ppermute | solution.py:301
  27.5 0.6 %collective-permute-start.6 = (bf16[1,40,128]{2,1,0:T(8,128)(2,1)S(1)}, bf16[1,40,128]{2,1,0:T(8,128)(2,1)S(1)}, u32[]{:S(2)}, u32[]{:S(2)}) collective-permute-start(bf16[1,40,128]{2,1,0:T(8,128)(2,1)S(1)} %get-tuple-element.28), channel_id=1, source_target_pairs={{0,12},{1,13},{2,14},{3,15},{4,8},{5,9},{6,10},{7,11},{8,4},{9,5},... | collective-permute-start | bytes 30728 | tf_op jit(solution)/shard_map/ppermute | solution.py:301
  28.1 3.1 %all-to-all-done.refs_0_ = bf16[16,200,128]{2,1,0:T(8,128)(2,1)S(1)} async-done(((bf16[16,200,128]{2,1,0:T(8,128)(2,1)}), bf16[16,200,128]{2,1,0:T(8,128)(2,1)S(1)}, u32[]{:S(2)}, u32[]{:S(2)}) %all-to-all-start) | async-done | bytes 819232 | tf_op jit(solution)/shard_map/all_to_all | solution.py:304
  31.2 0.0 copy-done.3
  31.2 1.6 %receive.1 = (bf16[16,192,128]{2,1,0:T(8,128)(2,1)}, f32[8,128]{1,0:T(8,128)S(1)}) custom-call(bf16[16,200,128]{2,1,0:T(8,128)(2,1)S(1)} %all-to-all-done.refs_0_, s32[1,16]{1,0:T(1,128)S(1)} %copy-done.3), custom_call_target="tpu_custom_call" | custom-call | tf_op jit(solution)/shard_map/receive/pallas_call | solution.py:258
  32.8 0.0 collective-permute-done.4.refs_2_
  32.8 1.5 %collective-permute-done.5.refs_3_ = bf16[1,40,128]{2,1,0:T(8,128)(2,1)S(1)} collective-permute-done((bf16[1,40,128]{2,1,0:T(8,128)(2,1)S(1)}, bf16[1,40,128]{2,1,0:T(8,128)(2,1)S(1)}, u32[]{:S(2)}, u32[]{:S(2)}) %collective-permute-start.5) | collective-permute-done | bytes 10272 | tf_op jit(solution)/shard_map/ppermute | solution.py:301
  34.2 0.0 collective-permute-done.6.refs_4_
  34.2 0.8 %finish.1 = (f32[16,24]{1,0:T(8,128)}, f32[16,256]{1,0:T(8,128)}) custom-call(f32[8,128]{1,0:T(8,128)S(1)} %get-tuple-element.19.refs_0_, f32[1,40,128]{2,1,0:T(8,128)S(1)} %get-tuple-element.25.refs_1_, bf16[1,40,128]{2,1,0:T(8,128)(2,1)S(1)} %collective-permute-done.4.refs_2_, bf16[1,40,128]{2,1,0:T(8,128)(2,1)S(1)} %collective-permute-done.5.refs_3_, ...), custom_call_target="tpu_custom_call" | custom-call | tf_op jit(solution)/shard_map/finish/pallas_call | solution.py:258
  (2 shorter events, 0.1 us)
Async XLA Ops:
  4.3 7.5 %copy-start = (bf16[8,256,192]{1,2,0:T(8,128)(2,1)S(1)}, bf16[8,256,192]{1,2,0:T(8,128)(2,1)}, u32[]{:S(2)}) copy-start(bf16[8,256,192]{1,2,0:T(8,128)(2,1)} %param.7) | copy-start | bytes 2359300
  4.3 7.5 %copy-start.1 = (bf16[8,256,192]{1,2,0:T(8,128)(2,1)S(1)}, bf16[8,256,192]{1,2,0:T(8,128)(2,1)}, u32[]{:S(2)}) copy-start(bf16[8,256,192]{1,2,0:T(8,128)(2,1)} %param.9) | copy-start | bytes 2359300
  4.3 26.9 %all-to-all-start = ((bf16[16,200,128]{2,1,0:T(8,128)(2,1)}), bf16[16,200,128]{2,1,0:T(8,128)(2,1)S(1)}, u32[]{:S(2)}, u32[]{:S(2)}) async-start(bf16[16,200,128]{2,1,0:T(8,128)(2,1)} %get-tuple-element.17), calls=%async_computation | async-start | bytes 1638400 | tf_op jit(solution)/shard_map/all_to_all | solution.py:304
  11.9 1.0 %copy-start.2 = (bf16[1536,128]{1,0:T(8,128)(2,1)S(1)}, bf16[1536,128]{1,0:T(8,128)(2,1)}, u32[]{:S(2)}) copy-start(bf16[1536,128]{1,0:T(8,128)(2,1)} %get-tuple-element.20.refs_3_) | copy-start | bytes 1179652
  13.4 1.5 %collective-permute-start = (f32[8,40,128]{2,1,0:T(8,128)S(1)}, f32[8,40,128]{2,1,0:T(8,128)S(1)}, u32[]{:S(2)}, u32[]{:S(2)}) collective-permute-start(f32[8,40,128]{2,1,0:T(8,128)S(1)} %get-tuple-element.22), channel_id=1, source_target_pairs={{0,1},{1,0},{2,3},{3,2},{4,5},{5,4},{6,7},{7,6},{8,9},{9,8},{10,11... | collective-permute-start | bytes 491528 | tf_op jit(solution)/shard_map/ppermute | solution.py:301
  15.0 5.2 %collective-permute-start.1 = (bf16[4,40,128]{2,1,0:T(8,128)(2,1)S(1)}, bf16[4,40,128]{2,1,0:T(8,128)(2,1)S(1)}, u32[]{:S(2)}, u32[]{:S(2)}) collective-permute-start(bf16[4,40,128]{2,1,0:T(8,128)(2,1)S(1)} %get-tuple-element.24), channel_id=1, source_target_pairs={{0,2},{1,3},{2,0},{3,1},{4,6},{5,7},{6,4},{7,5},{8,10},{9,11},{10,... | collective-permute-start | bytes 122888 | tf_op jit(solution)/shard_map/ppermute | solution.py:301
  16.9 4.0 %collective-permute-start.2 = (bf16[4,40,128]{2,1,0:T(8,128)(2,1)S(1)}, bf16[4,40,128]{2,1,0:T(8,128)(2,1)S(1)}, u32[]{:S(2)}, u32[]{:S(2)}) collective-permute-start(bf16[4,40,128]{2,1,0:T(8,128)(2,1)S(1)} %get-tuple-element.23.refs_1_), channel_id=1, source_target_pairs={{0,16},{1,17},{2,18},{3,19},{4,20},{5,21},{6,22},{7,23},{8,24},{9,... | collective-permute-start | bytes 122888 | tf_op jit(solution)/shard_map/ppermute | solution.py:301
  18.4 5.0 %collective-permute-start.3 = (bf16[4,40,128]{2,1,0:T(8,128)(2,1)S(1)}, bf16[4,40,128]{2,1,0:T(8,128)(2,1)S(1)}, u32[]{:S(2)}, u32[]{:S(2)}) collective-permute-start(bf16[4,40,128]{2,1,0:T(8,128)(2,1)S(1)} %get-tuple-element.24), channel_id=1, source_target_pairs={{0,18},{1,19},{2,16},{3,17},{4,22},{5,23},{6,20},{7,21},{8,26},{9,... | collective-permute-start | bytes 122888 | tf_op jit(solution)/shard_map/ppermute | solution.py:301
  23.5 9.3 %collective-permute-start.4 = (bf16[1,40,128]{2,1,0:T(8,128)(2,1)S(1)}, bf16[1,40,128]{2,1,0:T(8,128)(2,1)S(1)}, u32[]{:S(2)}, u32[]{:S(2)}) collective-permute-start(bf16[1,40,128]{2,1,0:T(8,128)(2,1)S(1)} %get-tuple-element.26), channel_id=1, source_target_pairs={{0,4},{1,5},{2,6},{3,7},{4,0},{5,1},{6,2},{7,3},{8,12},{9,13},{10,... | collective-permute-start | bytes 30728 | tf_op jit(solution)/shard_map/ppermute | solution.py:301
  25.6 5.6 %copy-start.3 = (s32[1,16]{1,0:T(1,128)S(1)}, s32[1,16]{1,0:T(1,128)}, u32[]{:S(2)}) copy-start(s32[1,16]{1,0:T(1,128)} %refs_1_.1) | copy-start | bytes 196
  25.6 8.6 %collective-permute-start.5 = (bf16[1,40,128]{2,1,0:T(8,128)(2,1)S(1)}, bf16[1,40,128]{2,1,0:T(8,128)(2,1)S(1)}, u32[]{:S(2)}, u32[]{:S(2)}) collective-permute-start(bf16[1,40,128]{2,1,0:T(8,128)(2,1)S(1)} %get-tuple-element.27), channel_id=1, source_target_pairs={{0,8},{1,9},{2,10},{3,11},{4,12},{5,13},{6,14},{7,15},{8,0},{9,1},... | collective-permute-start | bytes 30728 | tf_op jit(solution)/shard_map/ppermute | solution.py:301
  27.5 6.7 %collective-permute-start.6 = (bf16[1,40,128]{2,1,0:T(8,128)(2,1)S(1)}, bf16[1,40,128]{2,1,0:T(8,128)(2,1)S(1)}, u32[]{:S(2)}, u32[]{:S(2)}) collective-permute-start(bf16[1,40,128]{2,1,0:T(8,128)(2,1)S(1)} %get-tuple-element.28), channel_id=1, source_target_pairs={{0,12},{1,13},{2,14},{3,15},{4,8},{5,9},{6,10},{7,11},{8,4},{9,5},... | collective-permute-start | bytes 30728 | tf_op jit(solution)/shard_map/ppermute | solution.py:301

commit v4 on v3

--- a/solution.py
+++ b/solution.py
@@ -14,7 +14,10 @@
 HALF = 64
 CROSS = 0
 LAST = BF16
-STAGES = lambda bits: [[b] for b in range(1, bits - 2)] + [[bits - 2, bits - 1]]
+
+
+def STAGES(bits):
+    return [[b] for b in range(1, bits)]
 
 
 def dot(a, b, ca, cb):
@@ -38,18 +41,18 @@
     block = 8 * rank
     window = 2 * LANES
 
-    pairs = [(g_hbm, g_ref), (proj_hbm, proj_ref), (x_hbm, x_ref), (h_hbm, h_ref), (comp_hbm, comp_ref), (slot_hbm, slot_ref)]
-    copies = [pltpu.make_async_copy(a, b, sems.at[i]) for i, (a, b) in enumerate(pairs)]
-    pieces = 4
-    for i, (a, b) in enumerate(pairs[2:4]):
-        size = count // pieces
-        copies[2 + i] = [
-            pltpu.make_async_copy(
-                a.at[p * size:(p + 1) * size], b.at[p * size:(p + 1) * size], sems.at[8 + tables + i * pieces + p]
-            )
-            for p in range(pieces)
-        ]
-    for copy in copies[:2] + copies[2] + copies[3] + copies[4:]:
+    pairs = [(g_hbm, g_ref), (proj_hbm, proj_ref), (comp_hbm, comp_ref), (slot_hbm, slot_ref)]
+    small = [pltpu.make_async_copy(a, b, sems.at[i]) for i, (a, b) in enumerate(pairs)]
+    pieces = 2
+    size = count // pieces
+
+    def in_pieces(a, b, at):
+        parts = [pl.ds(p * size, size) for p in range(pieces)]
+        return [pltpu.make_async_copy(a.at[p], b.at[p], sems.at[at + i]) for i, p in enumerate(parts)]
+
+    x_copies = in_pieces(x_hbm, x_ref, 8 + tables)
+    h_copies = in_pieces(h_hbm, h_ref, 8 + tables + pieces)
+    for copy in small[:2] + x_copies + h_copies + small[2:]:
         copy.start()
     sends = [pltpu.make_async_copy(out_ref.at[t], out_hbm.at[t], sems.at[8 + t]) for t in range(tables)]
     both_copy = pltpu.make_async_copy(both, both_hbm, sems.at[6])
@@ -69,8 +72,8 @@
         masks.append((lane >= start + rank * sub) & (lane < start + rank * (sub + 1)))
     first = (iota((depth, LANES), 1) % HALF) < rank
 
-    copies[0].wait()
-    copies[1].wait()
+    small[0].wait()
+    small[1].wait()
     for a in range(width // 8):
         start, odd = (a * block) // LANES * LANES, a % 2
         piece = g_ref[:, start:start + window].astype(F32)
@@ -83,7 +86,7 @@
         halves = [dot(spread[i, lo:hi, :], folds[i], 1, 0).reshape(width // 16, 8, LANES) for i in range(2)]
         columns = jnp.stack(halves, axis=1).reshape(width, LANES)
         factors[s] = (columns + placed_proj).astype(BF16)
-    for copy in copies[2]:
+    for copy in x_copies:
         copy.wait()
     for s in range(count):
         terms = dot(x_ref[s], factors[s], 1, 0)
@@ -91,35 +94,36 @@
         split = jnp.where(first, high, terms - high)
         both[s * depth:(s + 1) * depth, :] = split.astype(BF16)
         swapped[s] = pltpu.roll(split, HALF, 1).astype(BF16)
-    for copy in copies[3]:
+    for copy in h_copies:
         copy.wait()
-    copies[4].wait()
-    copies[5].wait()
+    small[2].wait()
+    small[3].wait()
 
     both_copy.start()
 
     comp_t = comp_ref[...].astype(F32).T.astype(BF16)
-    for s in range(count):
-        h, other = h_ref[s], swapped[s]
-        h_wide = jnp.concatenate([h, h[LANES:]], axis=0)
-        other_wide = jnp.concatenate([other, other[LANES:]], axis=0)
-        grads = dot(comp_t, h_wide, 1, 1) + dot(factors[s], other_wide, 1, 1)
-        main[pl.ds(s, width, stride=count), :] = grads[:, :LANES]
-        rest[pl.ds(s, width, stride=count), :] = grads[:, LANES:]
-
     slot = slot_ref[...]
     slot_high = slot // 16
     sources = [slot_high.astype(F32), (slot - 16 * slot_high).astype(F32)]
     rows = local * count
     left = iota((rows // 2, LANES), 1) < HALF
-    for t in range(tables):
-        out_ref[t, 0:rows, :] = main[t * rows:(t + 1) * rows, :].astype(BF16)
-        upper = rest[t * rows:t * rows + rows // 2, :]
-        lower = rest[t * rows + rows // 2:(t + 1) * rows, :]
-        out_ref[t, rows:rows + rows // 2, :] = jnp.where(left, upper, lower).astype(BF16)
-        mixed = gather_lanes(sources, t, local)
-        out_ref[t, rows + rows // 2:, :] = mixed.astype(BF16)
-        sends[t].start()
+    span = width
+    for part in range(1):
+        begin, end = part * span, (part + 1) * span
+        for s in range(count):
+            h, other = h_ref[s], swapped[s]
+            h_wide = jnp.concatenate([h, h[LANES:]], axis=0)
+            other_wide = jnp.concatenate([other, other[LANES:]], axis=0)
+            grads = dot(comp_t[begin:end], h_wide, 1, 1) + dot(factors[s, begin:end], other_wide, 1, 1)
+            main[pl.ds(begin * count + s, span, stride=count), :] = grads[:, :LANES]
+            rest[pl.ds(begin * count + s, span, stride=count), :] = grads[:, LANES:]
+        for t in range(part * tables, (part + 1) * tables):
+            out_ref[t, 0:rows, :] = main[t * rows:(t + 1) * rows, :].astype(BF16)
+            upper = rest[t * rows:t * rows + rows // 2, :]
+            lower = rest[t * rows + rows // 2:(t + 1) * rows, :]
+            out_ref[t, rows:rows + rows // 2, :] = jnp.where(left, upper, lower).astype(BF16)
+            out_ref[t, rows + rows // 2:, :] = gather_lanes(sources, t, local).astype(BF16)
+            sends[t].start()
     for copy in [both_copy] + sends:
         copy.wait()
 

time: 35.3 us -> 34.9 us (0.989)
  waiting for transfers between devices: 10.5 us -> 8.89 us
  starting transfers between devices: 16.1 us -> 17.4 us
    all_to_all x1, waiting for transfers between devices: 3.11 us -> 0.03 us  [shards(): got = lax.all_to_all(sent, 'table', split_axis=0, concat_axis=0, tiled=True)]
    ppermute x7 -> x6, waiting for transfers between devices: 7.43 us -> 8.86 us  [swap(): return lax.ppermute(array, ('dp', 'table'), pairs)]
    ppermute x7 -> x6, starting transfers between devices: 8.61 us -> 9.92 us  [swap(): return lax.ppermute(array, ('dp', 'table'), pairs)]
    pallas_call x6 -> x7, Pallas kernels: 6.61 us -> 6.6 us  [call(): pl.pallas_call(body, out_shape=tuple((jax.ShapeDtypeStruct(*o) for o in o...]
  transfers between devices with their start and end apart: 8 -> 7, of which waited for: 6 -> 6; matrix products, arithmetic and copies ran while one was open for 0% -> 0% of each run, Pallas kernels for 6% -> 6%
where the time goes in v4:
time: 34.9 us; the launch traced here: 34.6 us
  starting transfers between devices  17.4 us (50%)
  waiting for transfers between devices  8.89 us (25%)
  Pallas kernels  6.6 us (19%)
  local copies, waits for them, and re-layouts  1.01 us (3%)
  between operations  0.73 us (2%)
    ppermute x6, starting transfers between devices, swap(): return lax.ppermute(array, ('dp', 'table'), pairs)  9.92 us
    ppermute x6, waiting for transfers between devices, swap(): return lax.ppermute(array, ('dp', 'table'), pairs)  8.86 us
    all_to_all x1, starting transfers between devices, shards(): got = lax.all_to_all(sent, 'table', split_axis=0, concat_axis=0, tiled=True)  7.5 us
    pallas_call x7, Pallas kernels, call(): pl.pallas_call(body, out_shape=tuple((jax.ShapeDtypeStruct(*o) for o in o...  6.6 us
    unnamed x8, local copies, waits for them, and re-layouts  1.01 us
  transfers between devices with their start and end apart: 7, of which 6 were waited for; matrix products, arithmetic and copies ran while one was open for 0% of the time, Pallas kernels for 6%

profile of v4, /device:TPU:0, one launch (start us, length us, event | category | flops | bytes accessed | tf_op | source)
XLA Modules:
  0.0 34.6 jit_solution(18438382781265552455)
XLA Ops:
  0.6 3.7 %send.1 = (bf16[16,200,128]{2,1,0:T(8,128)(2,1)}, bf16[1536,128]{1,0:T(8,128)(2,1)}) custom-call(bf16[8,192,256]{2,1,0:T(8,128)(2,1)} %bitcast.7, bf16[8,192,256]{2,1,0:T(8,128)(2,1)} %bitcast.9, bf16[8,6144]{1,0:T(8,128)(2,1)} %refs_2_.1, bf16[24,256]{1,0:T(8,128)(2,1)} %bitcast.11, bf16[256,256]{1,0:T(8,128)(2,1)} %refs_4_.1, s32[8,256]{1,0:T(8,128)} %refs_5_.1), custom_call_target="tpu_custom_call" | custom-call | tf_op jit(solution)/shard_map/send/pallas_call | solution.py:262
  4.3 0.0 copy-start
  4.3 0.0 copy-start.1
  4.3 7.5 %all-to-all-start = ((bf16[16,200,128]{2,1,0:T(8,128)(2,1)}), bf16[16,200,128]{2,1,0:T(8,128)(2,1)S(1)}, u32[]{:S(2)}, u32[]{:S(2)}) async-start(bf16[16,200,128]{2,1,0:T(8,128)(2,1)} %get-tuple-element.17), calls=%async_computation | async-start | bytes 1638400 | tf_op jit(solution)/shard_map/all_to_all | solution.py:308
  11.8 0.0 copy-done
  11.8 0.0 copy-done.1
  11.8 0.0 copy-start.2
  11.9 1.0 %copy-done.2 = bf16[1536,128]{1,0:T(8,128)(2,1)S(1)} copy-done((bf16[1536,128]{1,0:T(8,128)(2,1)S(1)}, bf16[1536,128]{1,0:T(8,128)(2,1)}, u32[]{:S(2)}) %copy-start.2) | copy-done | bytes 393240
  12.8 0.6 %weights.1 = (f32[8,40,128]{2,1,0:T(8,128)S(1)}, f32[8,40,128]{2,1,0:T(8,128)S(1)}) custom-call(s32[1]{0:T(128)} %bitcast.5.refs_0_, bf16[8,192,256]{2,1,0:T(8,128)(2,1)S(1)} %bitcast.8, bf16[8,192,256]{2,1,0:T(8,128)(2,1)S(1)} %bitcast.10, bf16[1536,128]{1,0:T(8,128)(2,1)S(1)} %copy-done.2), custom_call_target="tpu_custom_call" | custom-call | tf_op jit(solution)/shard_map/weights/pallas_call | solution.py:262
  13.4 0.5 %collective-permute-start = (f32[8,40,128]{2,1,0:T(8,128)S(1)}, f32[8,40,128]{2,1,0:T(8,128)S(1)}, u32[]{:S(2)}, u32[]{:S(2)}) collective-permute-start(f32[8,40,128]{2,1,0:T(8,128)S(1)} %get-tuple-element.22), channel_id=1, source_target_pairs={{0,1},{1,0},{2,3},{3,2},{4,5},{5,4},{6,7},{7,6},{8,9},{9,8},{10,11... | collective-permute-start | bytes 491528 | tf_op jit(solution)/shard_map/ppermute | solution.py:305
  13.9 1.0 %collective-permute-done.refs_2_ = f32[8,40,128]{2,1,0:T(8,128)S(1)} collective-permute-done((f32[8,40,128]{2,1,0:T(8,128)S(1)}, f32[8,40,128]{2,1,0:T(8,128)S(1)}, u32[]{:S(2)}, u32[]{:S(2)}) %collective-permute-start) | collective-permute-done | bytes 163872 | tf_op jit(solution)/shard_map/ppermute | solution.py:305
  15.0 1.9 %collective-permute-start.1 = (bf16[4,40,128]{2,1,0:T(8,128)(2,1)S(1)}, bf16[4,40,128]{2,1,0:T(8,128)(2,1)S(1)}, u32[]{:S(2)}, u32[]{:S(2)}) collective-permute-start(bf16[4,40,128]{2,1,0:T(8,128)(2,1)S(1)} %get-tuple-element.24), channel_id=1, source_target_pairs={{0,2},{1,3},{2,0},{3,1},{4,6},{5,7},{6,4},{7,5},{8,10},{9,11},{10,... | collective-permute-start | bytes 122888 | tf_op jit(solution)/shard_map/ppermute | solution.py:305
  16.9 1.5 %collective-permute-start.2 = (bf16[4,40,128]{2,1,0:T(8,128)(2,1)S(1)}, bf16[4,40,128]{2,1,0:T(8,128)(2,1)S(1)}, u32[]{:S(2)}, u32[]{:S(2)}) collective-permute-start(bf16[4,40,128]{2,1,0:T(8,128)(2,1)S(1)} %get-tuple-element.23.refs_1_), channel_id=1, source_target_pairs={{0,16},{1,17},{2,18},{3,19},{4,20},{5,21},{6,22},{7,23},{8,24},{9,... | collective-permute-start | bytes 122888 | tf_op jit(solution)/shard_map/ppermute | solution.py:305
  18.4 0.1 collective-permute-start.3
  18.5 1.7 %collective-permute-done.1.refs_2_ = bf16[4,40,128]{2,1,0:T(8,128)(2,1)S(1)} collective-permute-done((bf16[4,40,128]{2,1,0:T(8,128)(2,1)S(1)}, bf16[4,40,128]{2,1,0:T(8,128)(2,1)S(1)}, u32[]{:S(2)}, u32[]{:S(2)}) %collective-permute-start.1) | collective-permute-done | bytes 40992 | tf_op jit(solution)/shard_map/ppermute | solution.py:305
  20.2 0.7 %collective-permute-done.2.refs_3_ = bf16[4,40,128]{2,1,0:T(8,128)(2,1)S(1)} collective-permute-done((bf16[4,40,128]{2,1,0:T(8,128)(2,1)S(1)}, bf16[4,40,128]{2,1,0:T(8,128)(2,1)S(1)}, u32[]{:S(2)}, u32[]{:S(2)}) %collective-permute-start.2) | collective-permute-done | bytes 40992 | tf_op jit(solution)/shard_map/ppermute | solution.py:305
  20.9 2.5 %collective-permute-done.3.refs_4_ = bf16[4,40,128]{2,1,0:T(8,128)(2,1)S(1)} collective-permute-done((bf16[4,40,128]{2,1,0:T(8,128)(2,1)S(1)}, bf16[4,40,128]{2,1,0:T(8,128)(2,1)S(1)}, u32[]{:S(2)}, u32[]{:S(2)}) %collective-permute-start.3) | collective-permute-done | bytes 40992 | tf_op jit(solution)/shard_map/ppermute | solution.py:305
  23.5 2.1 %collective-permute-start.4 = (bf16[2,40,128]{2,1,0:T(8,128)(2,1)S(1)}, bf16[2,40,128]{2,1,0:T(8,128)(2,1)S(1)}, u32[]{:S(2)}, u32[]{:S(2)}) collective-permute-start(bf16[2,40,128]{2,1,0:T(8,128)(2,1)S(1)} %get-tuple-element.26), channel_id=1, source_target_pairs={{0,4},{1,5},{2,6},{3,7},{4,0},{5,1},{6,2},{7,3},{8,12},{9,13},{10,... | collective-permute-start | bytes 61448 | tf_op jit(solution)/shard_map/ppermute | solution.py:305
  25.6 1.8 %collective-permute-done.4.refs_2_ = bf16[2,40,128]{2,1,0:T(8,128)(2,1)S(1)} collective-permute-done((bf16[2,40,128]{2,1,0:T(8,128)(2,1)S(1)}, bf16[2,40,128]{2,1,0:T(8,128)(2,1)S(1)}, u32[]{:S(2)}, u32[]{:S(2)}) %collective-permute-start.4) | collective-permute-done | bytes 20512 | tf_op jit(solution)/shard_map/ppermute | solution.py:305
  27.4 0.0 copy-start.3
  27.4 3.8 %collective-permute-start.5 = (bf16[1,40,128]{2,1,0:T(8,128)(2,1)S(1)}, bf16[1,40,128]{2,1,0:T(8,128)(2,1)S(1)}, u32[]{:S(2)}, u32[]{:S(2)}) collective-permute-start(bf16[1,40,128]{2,1,0:T(8,128)(2,1)S(1)} %get-tuple-element.28), channel_id=1, source_target_pairs={{0,8},{1,9},{2,10},{3,11},{4,12},{5,13},{6,14},{7,15},{8,0},{9,1},... | collective-permute-start | bytes 30728 | tf_op jit(solution)/shard_map/ppermute | solution.py:305
  31.2 0.0 all-to-all-done.refs_0_
  31.2 0.0 copy-done.3
  31.2 1.6 %receive.1 = (bf16[16,192,128]{2,1,0:T(8,128)(2,1)}, f32[8,128]{1,0:T(8,128)S(1)}) custom-call(bf16[16,200,128]{2,1,0:T(8,128)(2,1)S(1)} %all-to-all-done.refs_0_, s32[1,16]{1,0:T(1,128)S(1)} %copy-done.3), custom_call_target="tpu_custom_call" | custom-call | tf_op jit(solution)/shard_map/receive/pallas_call | solution.py:262
  32.8 1.1 %collective-permute-done.5.refs_2_ = bf16[1,40,128]{2,1,0:T(8,128)(2,1)S(1)} collective-permute-done((bf16[1,40,128]{2,1,0:T(8,128)(2,1)S(1)}, bf16[1,40,128]{2,1,0:T(8,128)(2,1)S(1)}, u32[]{:S(2)}, u32[]{:S(2)}) %collective-permute-start.5) | collective-permute-done | bytes 10272 | tf_op jit(solution)/shard_map/ppermute | solution.py:305
  33.9 0.8 %finish.1 = (f32[16,24]{1,0:T(8,128)}, f32[16,256]{1,0:T(8,128)}) custom-call(f32[8,128]{1,0:T(8,128)S(1)} %get-tuple-element.19.refs_0_, f32[1,40,128]{2,1,0:T(8,128)S(1)} %get-tuple-element.27.refs_1_, bf16[1,40,128]{2,1,0:T(8,128)(2,1)S(1)} %collective-permute-done.5.refs_2_), custom_call_target="tpu_custom_call" | custom-call | tf_op jit(solution)/shard_map/finish/pallas_call | solution.py:262
  (3 shorter events, 0.1 us)
Async XLA Ops:
  4.3 7.5 %copy-start = (bf16[8,256,192]{1,2,0:T(8,128)(2,1)S(1)}, bf16[8,256,192]{1,2,0:T(8,128)(2,1)}, u32[]{:S(2)}) copy-start(bf16[8,256,192]{1,2,0:T(8,128)(2,1)} %param.7) | copy-start | bytes 2359300
  4.3 7.5 %copy-start.1 = (bf16[8,256,192]{1,2,0:T(8,128)(2,1)S(1)}, bf16[8,256,192]{1,2,0:T(8,128)(2,1)}, u32[]{:S(2)}) copy-start(bf16[8,256,192]{1,2,0:T(8,128)(2,1)} %param.9) | copy-start | bytes 2359300
  4.3 26.9 %all-to-all-start = ((bf16[16,200,128]{2,1,0:T(8,128)(2,1)}), bf16[16,200,128]{2,1,0:T(8,128)(2,1)S(1)}, u32[]{:S(2)}, u32[]{:S(2)}) async-start(bf16[16,200,128]{2,1,0:T(8,128)(2,1)} %get-tuple-element.17), calls=%async_computation | async-start | bytes 1638400 | tf_op jit(solution)/shard_map/all_to_all | solution.py:308
  11.8 1.0 %copy-start.2 = (bf16[1536,128]{1,0:T(8,128)(2,1)S(1)}, bf16[1536,128]{1,0:T(8,128)(2,1)}, u32[]{:S(2)}) copy-start(bf16[1536,128]{1,0:T(8,128)(2,1)} %get-tuple-element.20.refs_3_) | copy-start | bytes 1179652
  13.4 1.5 %collective-permute-start = (f32[8,40,128]{2,1,0:T(8,128)S(1)}, f32[8,40,128]{2,1,0:T(8,128)S(1)}, u32[]{:S(2)}, u32[]{:S(2)}) collective-permute-start(f32[8,40,128]{2,1,0:T(8,128)S(1)} %get-tuple-element.22), channel_id=1, source_target_pairs={{0,1},{1,0},{2,3},{3,2},{4,5},{5,4},{6,7},{7,6},{8,9},{9,8},{10,11... | collective-permute-start | bytes 491528 | tf_op jit(solution)/shard_map/ppermute | solution.py:305
  15.0 5.2 %collective-permute-start.1 = (bf16[4,40,128]{2,1,0:T(8,128)(2,1)S(1)}, bf16[4,40,128]{2,1,0:T(8,128)(2,1)S(1)}, u32[]{:S(2)}, u32[]{:S(2)}) collective-permute-start(bf16[4,40,128]{2,1,0:T(8,128)(2,1)S(1)} %get-tuple-element.24), channel_id=1, source_target_pairs={{0,2},{1,3},{2,0},{3,1},{4,6},{5,7},{6,4},{7,5},{8,10},{9,11},{10,... | collective-permute-start | bytes 122888 | tf_op jit(solution)/shard_map/ppermute | solution.py:305
  16.9 4.0 %collective-permute-start.2 = (bf16[4,40,128]{2,1,0:T(8,128)(2,1)S(1)}, bf16[4,40,128]{2,1,0:T(8,128)(2,1)S(1)}, u32[]{:S(2)}, u32[]{:S(2)}) collective-permute-start(bf16[4,40,128]{2,1,0:T(8,128)(2,1)S(1)} %get-tuple-element.23.refs_1_), channel_id=1, source_target_pairs={{0,16},{1,17},{2,18},{3,19},{4,20},{5,21},{6,22},{7,23},{8,24},{9,... | collective-permute-start | bytes 122888 | tf_op jit(solution)/shard_map/ppermute | solution.py:305
  18.4 5.0 %collective-permute-start.3 = (bf16[4,40,128]{2,1,0:T(8,128)(2,1)S(1)}, bf16[4,40,128]{2,1,0:T(8,128)(2,1)S(1)}, u32[]{:S(2)}, u32[]{:S(2)}) collective-permute-start(bf16[4,40,128]{2,1,0:T(8,128)(2,1)S(1)} %get-tuple-element.24), channel_id=1, source_target_pairs={{0,18},{1,19},{2,16},{3,17},{4,22},{5,23},{6,20},{7,21},{8,26},{9,... | collective-permute-start | bytes 122888 | tf_op jit(solution)/shard_map/ppermute | solution.py:305
  23.5 3.9 %collective-permute-start.4 = (bf16[2,40,128]{2,1,0:T(8,128)(2,1)S(1)}, bf16[2,40,128]{2,1,0:T(8,128)(2,1)S(1)}, u32[]{:S(2)}, u32[]{:S(2)}) collective-permute-start(bf16[2,40,128]{2,1,0:T(8,128)(2,1)S(1)} %get-tuple-element.26), channel_id=1, source_target_pairs={{0,4},{1,5},{2,6},{3,7},{4,0},{5,1},{6,2},{7,3},{8,12},{9,13},{10,... | collective-permute-start | bytes 61448 | tf_op jit(solution)/shard_map/ppermute | solution.py:305
  27.4 3.8 %copy-start.3 = (s32[1,16]{1,0:T(1,128)S(1)}, s32[1,16]{1,0:T(1,128)}, u32[]{:S(2)}) copy-start(s32[1,16]{1,0:T(1,128)} %refs_1_.1) | copy-start | bytes 196
  27.4 6.5 %collective-permute-start.5 = (bf16[1,40,128]{2,1,0:T(8,128)(2,1)S(1)}, bf16[1,40,128]{2,1,0:T(8,128)(2,1)S(1)}, u32[]{:S(2)}, u32[]{:S(2)}) collective-permute-start(bf16[1,40,128]{2,1,0:T(8,128)(2,1)S(1)} %get-tuple-element.28), channel_id=1, source_target_pairs={{0,8},{1,9},{2,10},{3,11},{4,12},{5,13},{6,14},{7,15},{8,0},{9,1},... | collective-permute-start | bytes 30728 | tf_op jit(solution)/shard_map/ppermute | solution.py:305

commit v5 on v4

--- a/solution.py
+++ b/solution.py
@@ -12,12 +12,12 @@
 BF16 = jnp.bfloat16
 LANES = 128
 HALF = 64
-CROSS = 0
-LAST = BF16
+CROSS = 1
+LAST = F32
 
 
 def STAGES(bits):
-    return [[b] for b in range(1, bits)]
+    return [[b] for b in range(bits - 1)]
 
 
 def dot(a, b, ca, cb):
@@ -32,8 +32,8 @@
     return -(-n // m) * m
 
 
-def send_kernel(tables, x_hbm, h_hbm, g_hbm, proj_hbm, comp_hbm, slot_hbm, out_hbm, both_hbm,
-                x_ref, h_ref, g_ref, proj_ref, comp_ref, slot_ref, spread, factors, both, swapped, main, rest, out_ref, sems):
+def send_kernel(tables, index_ref, x_hbm, h_hbm, g_hbm, proj_hbm, comp_hbm, slot_hbm, out_hbm, keep_hbm, give_hbm,
+                x_ref, h_ref, g_ref, proj_ref, comp_ref, slot_ref, spread, factors, both, swapped, main, rest, out_ref, keep_ref, give_ref, sems):
     count, depth, width = x_ref.shape
     rank = proj_ref.shape[0]
     comp_width = comp_ref.shape[0]
@@ -55,7 +55,9 @@
     for copy in small[:2] + x_copies + h_copies + small[2:]:
         copy.start()
     sends = [pltpu.make_async_copy(out_ref.at[t], out_hbm.at[t], sems.at[8 + t]) for t in range(tables)]
-    both_copy = pltpu.make_async_copy(both, both_hbm, sems.at[6])
+    part_copies = [
+        pltpu.make_async_copy(give_ref, give_hbm, sems.at[6]), pltpu.make_async_copy(keep_ref, keep_hbm, sems.at[7])
+    ]
 
     row, col = iota((rank, LANES), 0), iota((rank, LANES), 1)
     eye = ((col == row) | (col == row + rank)).astype(F32)
@@ -99,7 +101,14 @@
     small[2].wait()
     small[3].wait()
 
-    both_copy.start()
+    blocks = weight_blocks(tables, rank, x_ref, h_ref, both)
+    low = index_ref[0] < tables // 2
+    for i in range(tables // 2):
+        near, far = blocks[i], blocks[i + tables // 2]
+        keep_ref[i] = jnp.where(low, near, far)
+        give_ref[i] = jnp.where(low, far, near).astype(BF16)
+    for copy in part_copies:
+        copy.start()
 
     comp_t = comp_ref[...].astype(F32).T.astype(BF16)
     slot = slot_ref[...]
@@ -124,7 +133,7 @@
             out_ref[t, rows:rows + rows // 2, :] = jnp.where(left, upper, lower).astype(BF16)
             out_ref[t, rows + rows // 2:, :] = gather_lanes(sources, t, local).astype(BF16)
             sends[t].start()
-    for copy in [both_copy] + sends:
+    for copy in part_copies + sends:
         copy.wait()
 
 
@@ -141,7 +150,7 @@
     return mixed
 
 
-def weights_kernel(tables, rank, index_ref, x_ref, h_ref, both, keep_ref, give_ref):
+def weight_blocks(tables, rank, x_ref, h_ref, both):
     count, depth, width = x_ref.shape
     comp_width = h_ref.shape[2]
     local, comp_rows = width // tables, comp_width // tables
@@ -151,17 +160,13 @@
     proj_parts = dot(both[...], x_all, 0, 0)
     proj_grad = proj_parts[:rank] + proj_parts[rank:2 * rank]
     sources = [proj_grad[8 * i:8 * i + 8] for i in range(rank // 8)]
-    even = (index_ref[0] % 2) == 0
 
     def weight_block(t):
         mine = comp_grad[t * comp_rows:(t + 1) * comp_rows]
         pieces = [mine[:, i * LANES:(i + 1) * LANES] for i in range(width // LANES)]
         return jnp.concatenate(pieces + [gather_lanes(sources, t, local)], axis=0)
 
-    for i in range(tables // 2):
-        zero, one = weight_block(2 * i), weight_block(2 * i + 1)
-        keep_ref[i] = jnp.where(even, zero, one)
-        give_ref[i] = jnp.where(even, one, zero)
+    return [weight_block(t) for t in range(tables)]
 
 
 def split(blocks, bits, index):
@@ -192,9 +197,8 @@
     refs[-1][0] = total_of(refs[:-1], 0)
 
 
-def finish_kernel(scale, comp_rows, local, rank, after_ref, *refs):
-    proj_ref, comp_ref = refs[-2:]
-    total = total_of(refs[:-2], 0) * scale
+def write_weights(scale, comp_rows, local, rank, refs, proj_ref, comp_ref):
+    total = total_of(refs, 0) * scale
     halves = comp_ref.shape[1] // LANES
     comp_ref[...] = jnp.concatenate([total[i * comp_rows:(i + 1) * comp_rows] for i in range(halves)], axis=1)
     mixed = total[halves * comp_rows:halves * comp_rows + 8].T
@@ -205,8 +209,16 @@
     pass
 
 
-def receive_kernel(block_rows, in_ref, counts_ref, rows_hbm, after_ref, rows_ref, sems):
-    after_ref[...] = jnp.zeros_like(after_ref)
+def receive_kernel(block_rows, scale, rank, in_ref, counts_ref, *refs):
+    sums, (rows_hbm, proj_hbm, comp_hbm, rows_ref, proj_ref, comp_ref, sems) = refs[:-7], refs[-7:]
+    write_weights(scale, comp_ref.shape[0], rows_ref.shape[0], rank, sums, proj_ref, comp_ref)
+    pairs = rows_ref.shape[0] // 2
+    weights = [
+        pltpu.make_async_copy(proj_ref, proj_hbm, sems.at[pairs]),
+        pltpu.make_async_copy(comp_ref, comp_hbm, sems.at[pairs + 1]),
+    ]
+    for copy in weights:
+        copy.start()
     copies = []
     tables = in_ref.shape[0]
     local, depth, slots = rows_ref.shape
@@ -237,7 +249,7 @@
         pair = pl.ds(2 * j, 2)
         copies.append(pltpu.make_async_copy(rows_ref.at[pair], rows_hbm.at[pair], sems.at[j]))
         copies[j].start()
-    for copy in copies:
+    for copy in copies + weights:
         copy.wait()
 
 
@@ -272,13 +284,15 @@
     x, h = jnp.swapaxes(emb, 1, 2), jnp.swapaxes(grad_comp, 1, 2)
     index = lax.axis_index("table").astype(jnp.int32).reshape(1)
     part = comp_rows * (width // LANES) + 8
-    shapes = [((tables, total_rows, LANES), BF16), ((count * depth, LANES), BF16)]
-    sent, both = call(
+    shapes = [
+        ((tables, total_rows, LANES), BF16), ((tables // 2, part, LANES), F32), ((tables // 2, part, LANES), BF16)
+    ]
+    sent, keep, give = call(
         lambda *refs: send_kernel(tables, *refs),
         "send",
         shapes,
-        (x, h, grad_fm, proj.T, comp, slot),
-        [hbm] * 6,
+        (index, x, h, grad_fm, proj.T, comp, slot),
+        [smem] + [hbm] * 6,
         params=large,
         out=hbm,
         scratch_shapes=[
@@ -295,7 +309,7 @@
             pltpu.VMEM((count * width, LANES), F32),
             pltpu.VMEM((count * width, LANES), F32),
         ]
-        + [pltpu.VMEM(*shapes[0])]
+        + [pltpu.VMEM(*o) for o in shapes]
         + [pltpu.SemaphoreType.DMA((16 + tables,))],
     )
     def swap(array, offset, other_group=0):
@@ -305,26 +319,19 @@
         return lax.ppermute(array, ("dp", "table"), pairs)
 
     bits = tables.bit_length() - 1
+    sums = [keep, swap(give, tables // 2)]
     got = lax.all_to_all(sent, "table", split_axis=0, concat_axis=0, tiled=True)
-    keep, give = call(
-        lambda *refs: weights_kernel(tables, rank, *refs),
-        "weights",
-        [((tables // 2, part, LANES), F32)] * 2,
-        (index, x, h, both),
-        [smem] + [vmem] * 3,
-    )
-    sums = [keep, swap(give, 1)]
     for stage in STAGES(bits):
         size = sums[0].shape[0] >> len(stage)
         cross = stage == STAGES(bits)[CROSS] and groups == 2
-        kinds = [BF16 if cross else F32] + [BF16 if cross else LAST] * (2 ** len(stage) - 1)
+        kinds = [F32] + [LAST] * (2 ** len(stage) - 1)
         parts = call(
             lambda *refs, stage=stage: split_kernel(stage, *refs),
             "split",
             [((size, part, LANES), kind) for kind in kinds],
             (index, *sums),
             [smem] + [vmem] * len(sums),
-            cost_estimate=pl.CostEstimate(flops=10**6, bytes_accessed=10**6, transcendentals=0),
+            cost_estimate=pl.CostEstimate(flops=10**11 if stage == STAGES(bits)[0] else 10**6, bytes_accessed=10**6, transcendentals=0),
         )
         sums = [p if o == 0 else swap(p, o << stage[0]) for o, p in enumerate(parts)]
         if cross:
@@ -334,22 +341,20 @@
         keep, = call(add_kernel, "add", [(sums[0].shape, F32)], sums, [vmem] * len(sums))
         sums = [keep, swap(keep, 0, step)]
         step *= 2
-    row_grads, after = call(
-        lambda *refs: receive_kernel(slot_count // BLOCKS, *refs),
+    scale = 1.0 / math.sqrt(count * tables * groups * depth)
+    row_grads, grad_proj, grad_comp_out = call(
+        lambda *refs: receive_kernel(slot_count // BLOCKS, scale, rank, *refs),
         "receive",
-        [((local, depth, slot_count), BF16), ((8, LANES), F32)],
-        (got, counts),
-        [vmem] * 2,
-        out=(hbm, vmem),
-        scratch_shapes=[pltpu.VMEM((local, depth, slot_count), BF16), pltpu.SemaphoreType.DMA((local // 2,))],
-    )
-    scale = 1.0 / math.sqrt(count * tables * groups * depth)
-    grad_proj, grad_comp_out = call(
-        lambda *refs: finish_kernel(scale, comp_rows, local, rank, *refs),
-        "finish",
-        [((local, rank), F32), ((comp_rows, width), F32)],
-        (after, *sums),
-        [vmem] + [vmem] * len(sums),
+        [((local, depth, slot_count), BF16), ((local, rank), F32), ((comp_rows, width), F32)],
+        (got, counts, *sums),
+        [vmem] * (2 + len(sums)),
+        out=hbm,
+        scratch_shapes=[
+            pltpu.VMEM((local, depth, slot_count), BF16),
+            pltpu.VMEM((local, rank), F32),
+            pltpu.VMEM((comp_rows, width), F32),
+            pltpu.SemaphoreType.DMA((local // 2 + 2,)),
+        ],
     )
     return (jnp.swapaxes(row_grads, 1, 2)[None], grad_proj, grad_comp_out)
 

time: 34.9 us -> 34.2 us (0.980)
  waiting for transfers between devices: 8.89 us -> 13.7 us
  starting transfers between devices: 17.4 us -> 13.7 us
  local copies, waits for them, and re-layouts: 1.01 us -> 0.01 us
  Pallas kernels: 6.6 us -> 5.77 us
    all_to_all x1, waiting for transfers between devices: 0.03 us -> 4.42 us  [shards(): got = lax.all_to_all(sent, 'table', split_axis=0, concat_axis=0, tiled=True)]
    all_to_all x1, starting transfers between devices: 7.5 us -> 4.01 us  [shards(): got = lax.all_to_all(sent, 'table', split_axis=0, concat_axis=0, tiled=True)]
    unnamed x8 -> x4, local copies, waits for them, and re-layouts: 1.01 us -> 0.01 us
    pallas_call x7 -> x5, Pallas kernels: 6.6 us -> 5.77 us  [call(): pl.pallas_call(body, out_shape=tuple((jax.ShapeDtypeStruct(*o) for o in o...]
    ppermute x6, waiting for transfers between devices: 8.86 us -> 9.25 us  [swap(): return lax.ppermute(array, ('dp', 'table'), pairs)]
  transfers between devices with their start and end apart: 7 -> 7, of which waited for: 6 -> 6; matrix products, arithmetic and copies ran while one was open for 0% -> 0% of each run, Pallas kernels for 6% -> 0%
where the time goes in v5:
time: 34.2 us; the launch traced here: 33.9 us
  starting transfers between devices  13.7 us (40%)
  waiting for transfers between devices  13.7 us (40%)
  Pallas kernels  5.77 us (17%)
  between operations  0.68 us (2%)
    ppermute x6, starting transfers between devices, swap(): return lax.ppermute(array, ('dp', 'table'), pairs)  9.7 us
    ppermute x6, waiting for transfers between devices, swap(): return lax.ppermute(array, ('dp', 'table'), pairs)  9.25 us
    pallas_call x5, Pallas kernels, call(): pl.pallas_call(body, out_shape=tuple((jax.ShapeDtypeStruct(*o) for o in o...  5.77 us
    all_to_all x1, waiting for transfers between devices, shards(): got = lax.all_to_all(sent, 'table', split_axis=0, concat_axis=0, tiled=True)  4.42 us
    all_to_all x1, starting transfers between devices, shards(): got = lax.all_to_all(sent, 'table', split_axis=0, concat_axis=0, tiled=True)  4.01 us
  transfers between devices with their start and end apart: 7, of which 6 were waited for; matrix products, arithmetic and copies ran while one was open for 0% of the time, Pallas kernels for 0%

profile of v5, /device:TPU:0, one launch (start us, length us, event | category | flops | bytes accessed | tf_op | source)
XLA Modules:
  0.0 33.9 jit_solution(638682452695340791)
XLA Ops:
  0.6 4.1 %send.1 = (bf16[16,200,128]{2,1,0:T(8,128)(2,1)}, f32[8,40,128]{2,1,0:T(8,128)}, bf16[8,40,128]{2,1,0:T(8,128)(2,1)}) custom-call(s32[1]{0:T(128)} %bitcast.refs_0_, bf16[8,192,256]{2,1,0:T(8,128)(2,1)} %bitcast.7, bf16[8,192,256]{2,1,0:T(8,128)(2,1)} %bitcast.8, bf16[8,6144]{1,0:T(8,128)(2,1)} %refs_3_.1, bf16[24,256]{1,0:T(8,128)(2,1)} %bitcast.9, ...), custom_call_target="tpu_custom_call" | custom-call | tf_op jit(solution)/shard_map/send/pallas_call | solution.py:274
  4.7 4.1 %collective-permute-start = (bf16[8,40,128]{2,1,0:T(8,128)(2,1)}, bf16[8,40,128]{2,1,0:T(8,128)(2,1)S(1)}, u32[]{:S(2)}, u32[]{:S(2)}) collective-permute-start(bf16[8,40,128]{2,1,0:T(8,128)(2,1)} %get-tuple-element.17), channel_id=1, source_target_pairs={{0,8},{1,9},{2,10},{3,11},{4,12},{5,13},{6,14},{7,15},{8,0},{9,1},... | collective-permute-start | bytes 245768 | tf_op jit(solution)/shard_map/ppermute | solution.py:319
  8.8 0.0 copy-start.1
  8.8 4.0 %all-to-all-start = ((bf16[16,200,128]{2,1,0:T(8,128)(2,1)}), bf16[16,200,128]{2,1,0:T(8,128)(2,1)S(1)}, u32[]{:S(2)}, u32[]{:S(2)}) async-start(bf16[16,200,128]{2,1,0:T(8,128)(2,1)} %get-tuple-element.15), calls=%async_computation | async-start | bytes 1638400 | tf_op jit(solution)/shard_map/all_to_all | solution.py:323
  12.8 0.4 %collective-permute-done.refs_2_ = bf16[8,40,128]{2,1,0:T(8,128)(2,1)S(1)} collective-permute-done((bf16[8,40,128]{2,1,0:T(8,128)(2,1)}, bf16[8,40,128]{2,1,0:T(8,128)(2,1)S(1)}, u32[]{:S(2)}, u32[]{:S(2)}) %collective-permute-start) | collective-permute-done | bytes 81952 | tf_op jit(solution)/shard_map/ppermute | solution.py:319
  13.2 0.0 copy-done.1
  13.3 0.1 collective-permute-start.1
  13.4 1.2 %collective-permute-done.1.refs_2_ = f32[4,40,128]{2,1,0:T(8,128)S(1)} collective-permute-done((f32[4,40,128]{2,1,0:T(8,128)S(1)}, f32[4,40,128]{2,1,0:T(8,128)S(1)}, u32[]{:S(2)}, u32[]{:S(2)}) %collective-permute-start.1) | collective-permute-done | bytes 81952 | tf_op jit(solution)/shard_map/ppermute | solution.py:319
  14.6 1.7 %collective-permute-start.2 = (f32[2,40,128]{2,1,0:T(8,128)S(1)}, f32[2,40,128]{2,1,0:T(8,128)S(1)}, u32[]{:S(2)}, u32[]{:S(2)}) collective-permute-start(f32[2,40,128]{2,1,0:T(8,128)S(1)} %get-tuple-element.21), channel_id=1, source_target_pairs={{0,2},{1,3},{2,0},{3,1},{4,6},{5,7},{6,4},{7,5},{8,10},{9,11},{10,... | collective-permute-start | bytes 122888 | tf_op jit(solution)/shard_map/ppermute | solution.py:319
  16.4 1.5 %collective-permute-start.3 = (f32[2,40,128]{2,1,0:T(8,128)S(1)}, f32[2,40,128]{2,1,0:T(8,128)S(1)}, u32[]{:S(2)}, u32[]{:S(2)}) collective-permute-start(f32[2,40,128]{2,1,0:T(8,128)S(1)} %get-tuple-element.20.refs_1_), channel_id=1, source_target_pairs={{0,16},{1,17},{2,18},{3,19},{4,20},{5,21},{6,22},{7,23},{8,24},{9,... | collective-permute-start | bytes 122888 | tf_op jit(solution)/shard_map/ppermute | solution.py:319
  17.9 0.3 collective-permute-start.4
  18.2 4.1 %collective-permute-done.2.refs_2_ = f32[2,40,128]{2,1,0:T(8,128)S(1)} collective-permute-done((f32[2,40,128]{2,1,0:T(8,128)S(1)}, f32[2,40,128]{2,1,0:T(8,128)S(1)}, u32[]{:S(2)}, u32[]{:S(2)}) %collective-permute-start.2) | collective-permute-done | bytes 40992 | tf_op jit(solution)/shard_map/ppermute | solution.py:319
  22.2 0.0 collective-permute-done.3.refs_3_
  22.2 1.7 %collective-permute-done.4.refs_4_ = f32[2,40,128]{2,1,0:T(8,128)S(1)} collective-permute-done((f32[2,40,128]{2,1,0:T(8,128)S(1)}, f32[2,40,128]{2,1,0:T(8,128)S(1)}, u32[]{:S(2)}, u32[]{:S(2)}) %collective-permute-start.4) | collective-permute-done | bytes 40992 | tf_op jit(solution)/shard_map/ppermute | solution.py:319
  23.9 0.0 copy-start
  23.9 1.9 %collective-permute-start.5 = (f32[1,40,128]{2,1,0:T(8,128)S(1)}, f32[1,40,128]{2,1,0:T(8,128)S(1)}, u32[]{:S(2)}, u32[]{:S(2)}) collective-permute-start(f32[1,40,128]{2,1,0:T(8,128)S(1)} %get-tuple-element.23), channel_id=1, source_target_pairs={{0,4},{1,5},{2,6},{3,7},{4,0},{5,1},{6,2},{7,3},{8,12},{9,13},{10,... | collective-permute-start | bytes 61448 | tf_op jit(solution)/shard_map/ppermute | solution.py:319
  25.9 1.9 %collective-permute-done.5.refs_3_ = f32[1,40,128]{2,1,0:T(8,128)S(1)} collective-permute-done((f32[1,40,128]{2,1,0:T(8,128)S(1)}, f32[1,40,128]{2,1,0:T(8,128)S(1)}, u32[]{:S(2)}, u32[]{:S(2)}) %collective-permute-start.5) | collective-permute-done | bytes 20512 | tf_op jit(solution)/shard_map/ppermute | solution.py:319
  27.8 4.4 %all-to-all-done.refs_0_ = bf16[16,200,128]{2,1,0:T(8,128)(2,1)S(1)} async-done(((bf16[16,200,128]{2,1,0:T(8,128)(2,1)}), bf16[16,200,128]{2,1,0:T(8,128)(2,1)S(1)}, u32[]{:S(2)}, u32[]{:S(2)}) %all-to-all-start) | async-done | bytes 819232 | tf_op jit(solution)/shard_map/all_to_all | solution.py:323
  32.2 0.0 copy-done
  32.2 1.7 %receive.1 = (bf16[16,192,128]{2,1,0:T(8,128)(2,1)}, f32[16,24]{1,0:T(8,128)}, f32[16,256]{1,0:T(8,128)}) custom-call(bf16[16,200,128]{2,1,0:T(8,128)(2,1)S(1)} %all-to-all-done.refs_0_, s32[1,16]{1,0:T(1,128)S(1)} %copy-done, f32[1,40,128]{2,1,0:T(8,128)S(1)} %get-tuple-element.22.refs_2_, f32[1,40,128]{2,1,0:T(8,128)S(1)} %collective-permute-done.5.refs_3_), custom_call_target="tpu_custom_call" | custom-call | tf_op jit(solution)/shard_map/receive/pallas_call | solution.py:274
  (3 shorter events, 0.1 us)
Async XLA Ops:
  4.7 8.5 %collective-permute-start = (bf16[8,40,128]{2,1,0:T(8,128)(2,1)}, bf16[8,40,128]{2,1,0:T(8,128)(2,1)S(1)}, u32[]{:S(2)}, u32[]{:S(2)}) collective-permute-start(bf16[8,40,128]{2,1,0:T(8,128)(2,1)} %get-tuple-element.17), channel_id=1, source_target_pairs={{0,8},{1,9},{2,10},{3,11},{4,12},{5,13},{6,14},{7,15},{8,0},{9,1},... | collective-permute-start | bytes 245768 | tf_op jit(solution)/shard_map/ppermute | solution.py:319
  8.8 4.4 %copy-start.1 = (f32[8,40,128]{2,1,0:T(8,128)S(1)}, f32[8,40,128]{2,1,0:T(8,128)}, u32[]{:S(2)}) copy-start(f32[8,40,128]{2,1,0:T(8,128)} %get-tuple-element.16.refs_1_) | copy-start | bytes 491524
  8.8 23.4 %all-to-all-start = ((bf16[16,200,128]{2,1,0:T(8,128)(2,1)}), bf16[16,200,128]{2,1,0:T(8,128)(2,1)S(1)}, u32[]{:S(2)}, u32[]{:S(2)}) async-start(bf16[16,200,128]{2,1,0:T(8,128)(2,1)} %get-tuple-element.15), calls=%async_computation | async-start | bytes 1638400 | tf_op jit(solution)/shard_map/all_to_all | solution.py:323
  13.3 1.3 %collective-permute-start.1 = (f32[4,40,128]{2,1,0:T(8,128)S(1)}, f32[4,40,128]{2,1,0:T(8,128)S(1)}, u32[]{:S(2)}, u32[]{:S(2)}) collective-permute-start(f32[4,40,128]{2,1,0:T(8,128)S(1)} %get-tuple-element.19), channel_id=1, source_target_pairs={{0,1},{1,0},{2,3},{3,2},{4,5},{5,4},{6,7},{7,6},{8,9},{9,8},{10,11... | collective-permute-start | bytes 245768 | tf_op jit(solution)/shard_map/ppermute | solution.py:319
  14.6 7.6 %collective-permute-start.2 = (f32[2,40,128]{2,1,0:T(8,128)S(1)}, f32[2,40,128]{2,1,0:T(8,128)S(1)}, u32[]{:S(2)}, u32[]{:S(2)}) collective-permute-start(f32[2,40,128]{2,1,0:T(8,128)S(1)} %get-tuple-element.21), channel_id=1, source_target_pairs={{0,2},{1,3},{2,0},{3,1},{4,6},{5,7},{6,4},{7,5},{8,10},{9,11},{10,... | collective-permute-start | bytes 122888 | tf_op jit(solution)/shard_map/ppermute | solution.py:319
  16.4 5.9 %collective-permute-start.3 = (f32[2,40,128]{2,1,0:T(8,128)S(1)}, f32[2,40,128]{2,1,0:T(8,128)S(1)}, u32[]{:S(2)}, u32[]{:S(2)}) collective-permute-start(f32[2,40,128]{2,1,0:T(8,128)S(1)} %get-tuple-element.20.refs_1_), channel_id=1, source_target_pairs={{0,16},{1,17},{2,18},{3,19},{4,20},{5,21},{6,22},{7,23},{8,24},{9,... | collective-permute-start | bytes 122888 | tf_op jit(solution)/shard_map/ppermute | solution.py:319
  17.9 6.0 %collective-permute-start.4 = (f32[2,40,128]{2,1,0:T(8,128)S(1)}, f32[2,40,128]{2,1,0:T(8,128)S(1)}, u32[]{:S(2)}, u32[]{:S(2)}) collective-permute-start(f32[2,40,128]{2,1,0:T(8,128)S(1)} %get-tuple-element.21), channel_id=1, source_target_pairs={{0,18},{1,19},{2,16},{3,17},{4,22},{5,23},{6,20},{7,21},{8,26},{9,... | collective-permute-start | bytes 122888 | tf_op jit(solution)/shard_map/ppermute | solution.py:319
  23.9 8.3 %copy-start = (s32[1,16]{1,0:T(1,128)S(1)}, s32[1,16]{1,0:T(1,128)}, u32[]{:S(2)}) copy-start(s32[1,16]{1,0:T(1,128)} %refs_1_.1) | copy-start | bytes 196
  23.9 3.8 %collective-permute-start.5 = (f32[1,40,128]{2,1,0:T(8,128)S(1)}, f32[1,40,128]{2,1,0:T(8,128)S(1)}, u32[]{:S(2)}, u32[]{:S(2)}) collective-permute-start(f32[1,40,128]{2,1,0:T(8,128)S(1)} %get-tuple-element.23), channel_id=1, source_target_pairs={{0,4},{1,5},{2,6},{3,7},{4,0},{5,1},{6,2},{7,3},{8,12},{9,13},{10,... | collective-permute-start | bytes 61448 | tf_op jit(solution)/shard_map/ppermute | solution.py:319

commit v6 on v5

--- a/solution.py
+++ b/solution.py
@@ -32,8 +32,8 @@
     return -(-n // m) * m
 
 
-def send_kernel(tables, index_ref, x_hbm, h_hbm, g_hbm, proj_hbm, comp_hbm, slot_hbm, out_hbm, keep_hbm, give_hbm,
-                x_ref, h_ref, g_ref, proj_ref, comp_ref, slot_ref, spread, factors, both, swapped, main, rest, out_ref, keep_ref, give_ref, sems):
+def send_kernel(tables, index_ref, x_hbm, h_hbm, g_hbm, proj_hbm, comp_hbm, slot_hbm, out_hbm, both_hbm, give_hbm,
+                x_ref, h_ref, g_ref, proj_ref, comp_ref, slot_ref, spread, factors, both, swapped, main, rest, out_ref, give_ref, sems):
     count, depth, width = x_ref.shape
     rank = proj_ref.shape[0]
     comp_width = comp_ref.shape[0]
@@ -56,7 +56,7 @@
         copy.start()
     sends = [pltpu.make_async_copy(out_ref.at[t], out_hbm.at[t], sems.at[8 + t]) for t in range(tables)]
     part_copies = [
-        pltpu.make_async_copy(give_ref, give_hbm, sems.at[6]), pltpu.make_async_copy(keep_ref, keep_hbm, sems.at[7])
+        pltpu.make_async_copy(give_ref, give_hbm, sems.at[6]), pltpu.make_async_copy(both, both_hbm, sems.at[7])
     ]
 
     row, col = iota((rank, LANES), 0), iota((rank, LANES), 1)
@@ -101,12 +101,9 @@
     small[2].wait()
     small[3].wait()
 
-    blocks = weight_blocks(tables, rank, x_ref, h_ref, both)
-    low = index_ref[0] < tables // 2
-    for i in range(tables // 2):
-        near, far = blocks[i], blocks[i + tables // 2]
-        keep_ref[i] = jnp.where(low, near, far)
-        give_ref[i] = jnp.where(low, far, near).astype(BF16)
+    half = 1 - index_ref[0] // (tables // 2)
+    for i, block in enumerate(half_blocks(tables, rank, x_ref, h_ref, both, half)):
+        give_ref[i] = block.astype(BF16)
     for copy in part_copies:
         copy.start()
 
@@ -150,23 +147,32 @@
     return mixed
 
 
-def weight_blocks(tables, rank, x_ref, h_ref, both):
+def half_blocks(tables, rank, x_ref, h_ref, both, half):
     count, depth, width = x_ref.shape
     comp_width = h_ref.shape[2]
     local, comp_rows = width // tables, comp_width // tables
+    h_lanes = pl.ds(pl.multiple_of(half * (comp_width // 2), LANES), comp_width // 2)
+    x_lanes = pl.ds(pl.multiple_of(half * (width // 2), LANES), width // 2)
     x_all = x_ref[...].reshape(count * depth, width)
-    h_all = h_ref[...].reshape(count * depth, comp_width)
-    comp_grad = dot(h_all, x_all, 0, 0)
-    proj_parts = dot(both[...], x_all, 0, 0)
+    h_half = h_ref[:, :, h_lanes].reshape(count * depth, comp_width // 2)
+    x_half = x_ref[:, :, x_lanes].reshape(count * depth, width // 2)
+    comp_grad = dot(h_half, x_all, 0, 0)
+    proj_parts = dot(both[...], x_half, 0, 0)
     proj_grad = proj_parts[:rank] + proj_parts[rank:2 * rank]
     sources = [proj_grad[8 * i:8 * i + 8] for i in range(rank // 8)]
 
-    def weight_block(t):
+    def block(t):
         mine = comp_grad[t * comp_rows:(t + 1) * comp_rows]
         pieces = [mine[:, i * LANES:(i + 1) * LANES] for i in range(width // LANES)]
         return jnp.concatenate(pieces + [gather_lanes(sources, t, local)], axis=0)
 
-    return [weight_block(t) for t in range(tables)]
+    return [block(t) for t in range(tables // 2)]
+
+
+def keep_kernel(tables, rank, index_ref, x_ref, h_ref, both, keep_ref):
+    half = index_ref[0] // (tables // 2)
+    for i, block in enumerate(half_blocks(tables, rank, x_ref, h_ref, both, half)):
+        keep_ref[i] = block
 
 
 def split(blocks, bits, index):
@@ -285,9 +291,9 @@
     index = lax.axis_index("table").astype(jnp.int32).reshape(1)
     part = comp_rows * (width // LANES) + 8
     shapes = [
-        ((tables, total_rows, LANES), BF16), ((tables // 2, part, LANES), F32), ((tables // 2, part, LANES), BF16)
+        ((tables, total_rows, LANES), BF16), ((count * depth, LANES), BF16), ((tables // 2, part, LANES), BF16)
     ]
-    sent, keep, give = call(
+    sent, both, give = call(
         lambda *refs: send_kernel(tables, *refs),
         "send",
         shapes,
@@ -309,7 +315,7 @@
             pltpu.VMEM((count * width, LANES), F32),
             pltpu.VMEM((count * width, LANES), F32),
         ]
-        + [pltpu.VMEM(*o) for o in shapes]
+        + [pltpu.VMEM(*shapes[0]), pltpu.VMEM(*shapes[2])]
         + [pltpu.SemaphoreType.DMA((16 + tables,))],
     )
     def swap(array, offset, other_group=0):
@@ -319,8 +325,16 @@
         return lax.ppermute(array, ("dp", "table"), pairs)
 
     bits = tables.bit_length() - 1
-    sums = [keep, swap(give, tables // 2)]
+    taken = swap(give, tables // 2)
     got = lax.all_to_all(sent, "table", split_axis=0, concat_axis=0, tiled=True)
+    keep, = call(
+        lambda *refs: keep_kernel(tables, rank, *refs),
+        "keep",
+        [((tables // 2, part, LANES), F32)],
+        (index, x, h, both),
+        [smem] + [vmem] * 3,
+    )
+    sums = [keep, taken]
     for stage in STAGES(bits):
         size = sums[0].shape[0] >> len(stage)
         cross = stage == STAGES(bits)[CROSS] and groups == 2

time: 34.2 us -> 34.1 us (level)
  waiting for transfers between devices: 13.7 us -> 11.5 us
  local copies, waits for them, and re-layouts: 0.01 us -> 1 us
  starting transfers between devices: 13.7 us -> 14.4 us
    ppermute x6, waiting for transfers between devices: 9.25 us -> 7.56 us  [swap(): return lax.ppermute(array, ('dp', 'table'), pairs)]
    unnamed x4 -> x8, local copies, waits for them, and re-layouts: 0.01 us -> 1 us
    ppermute x6, starting transfers between devices: 9.7 us -> 10.4 us  [swap(): return lax.ppermute(array, ('dp', 'table'), pairs)]
    all_to_all x1, waiting for transfers between devices: 4.42 us -> 3.92 us  [shards(): got = lax.all_to_all(sent, 'table', split_axis=0, concat_axis=0, tiled=True)]
    pallas_call x5 -> x6, Pallas kernels: 5.77 us -> 6.09 us  [call(): pl.pallas_call(body, out_shape=tuple((jax.ShapeDtypeStruct(*o) for o in o...]
  transfers between devices with their start and end apart: 7 -> 7, of which waited for: 6 -> 6; matrix products, arithmetic and copies ran while one was open for 0% -> 0% of each run, Pallas kernels for 0% -> 1%
where the time goes in v6:
time: 34.1 us; the launch traced here: 33.7 us
  starting transfers between devices  14.4 us (42%)
  waiting for transfers between devices  11.5 us (34%)
  Pallas kernels  6.09 us (18%)
  local copies, waits for them, and re-layouts  1 us (3%)
  between operations  0.72 us (2%)
    ppermute x6, starting transfers between devices, swap(): return lax.ppermute(array, ('dp', 'table'), pairs)  10.4 us
    ppermute x6, waiting for transfers between devices, swap(): return lax.ppermute(array, ('dp', 'table'), pairs)  7.56 us
    pallas_call x6, Pallas kernels, call(): pl.pallas_call(body, out_shape=tuple((jax.ShapeDtypeStruct(*o) for o in o...  6.09 us
    all_to_all x1, starting transfers between devices, shards(): got = lax.all_to_all(sent, 'table', split_axis=0, concat_axis=0, tiled=True)  4.02 us
    all_to_all x1, waiting for transfers between devices, shards(): got = lax.all_to_all(sent, 'table', split_axis=0, concat_axis=0, tiled=True)  3.92 us
    unnamed x8, local copies, waits for them, and re-layouts  1 us
  transfers between devices with their start and end apart: 7, of which 6 were waited for; matrix products, arithmetic and copies ran while one was open for 0% of the time, Pallas kernels for 1%

profile of v6, /device:TPU:0, one launch (start us, length us, event | category | flops | bytes accessed | tf_op | source)
XLA Modules:
  0.0 33.7 jit_solution(4776094703260987825)
XLA Ops:
  0.6 3.9 %send.1 = (bf16[16,200,128]{2,1,0:T(8,128)(2,1)}, bf16[1536,128]{1,0:T(8,128)(2,1)}, bf16[8,40,128]{2,1,0:T(8,128)(2,1)}) custom-call(s32[1]{0:T(128)} %bitcast.refs_0_, bf16[8,192,256]{2,1,0:T(8,128)(2,1)} %bitcast.7, bf16[8,192,256]{2,1,0:T(8,128)(2,1)} %bitcast.9, bf16[8,6144]{1,0:T(8,128)(2,1)} %refs_3_.1, bf16[24,256]{1,0:T(8,128)(2,1)} %bitcast.11, ...), custom_call_target="tpu_custom_call" | custom-call | tf_op jit(solution)/shard_map/send/pallas_call | solution.py:280
  4.6 4.1 %collective-permute-start = (bf16[8,40,128]{2,1,0:T(8,128)(2,1)}, bf16[8,40,128]{2,1,0:T(8,128)(2,1)S(1)}, u32[]{:S(2)}, u32[]{:S(2)}) collective-permute-start(bf16[8,40,128]{2,1,0:T(8,128)(2,1)} %get-tuple-element.17), channel_id=1, source_target_pairs={{0,8},{1,9},{2,10},{3,11},{4,12},{5,13},{6,14},{7,15},{8,0},{9,1},... | collective-permute-start | bytes 245768 | tf_op jit(solution)/shard_map/ppermute | solution.py:325
  8.7 0.0 copy-start
  8.7 0.0 copy-start.1
  8.7 4.0 %all-to-all-start = ((bf16[16,200,128]{2,1,0:T(8,128)(2,1)}), bf16[16,200,128]{2,1,0:T(8,128)(2,1)S(1)}, u32[]{:S(2)}, u32[]{:S(2)}) async-start(bf16[16,200,128]{2,1,0:T(8,128)(2,1)} %get-tuple-element.15), calls=%async_computation | async-start | bytes 1638400 | tf_op jit(solution)/shard_map/all_to_all | solution.py:329
  12.7 0.0 copy-done
  12.7 0.0 copy-done.1
  12.7 0.0 copy-start.2
  12.7 1.0 %copy-done.2 = bf16[1536,128]{1,0:T(8,128)(2,1)S(1)} copy-done((bf16[1536,128]{1,0:T(8,128)(2,1)S(1)}, bf16[1536,128]{1,0:T(8,128)(2,1)}, u32[]{:S(2)}) %copy-start.2) | copy-done | bytes 393240
  13.7 0.5 %keep.1.refs_1_ = f32[8,40,128]{2,1,0:T(8,128)S(1)} custom-call(s32[1]{0:T(128)} %bitcast.refs_0_, bf16[8,192,256]{2,1,0:T(8,128)(2,1)S(1)} %bitcast.8, bf16[8,192,256]{2,1,0:T(8,128)(2,1)S(1)} %bitcast.10, bf16[1536,128]{1,0:T(8,128)(2,1)S(1)} %copy-done.2), custom_call_target="tpu_custom_call" | custom-call | tf_op jit(solution)/shard_map/keep/pallas_call | solution.py:280
  14.2 0.0 collective-permute-done.refs_2_
  14.2 0.5 %collective-permute-start.1 = (f32[4,40,128]{2,1,0:T(8,128)S(1)}, f32[4,40,128]{2,1,0:T(8,128)S(1)}, u32[]{:S(2)}, u32[]{:S(2)}) collective-permute-start(f32[4,40,128]{2,1,0:T(8,128)S(1)} %get-tuple-element.19), channel_id=1, source_target_pairs={{0,1},{1,0},{2,3},{3,2},{4,5},{5,4},{6,7},{7,6},{8,9},{9,8},{10,11... | collective-permute-start | bytes 245768 | tf_op jit(solution)/shard_map/ppermute | solution.py:325
  14.7 0.9 %collective-permute-done.1.refs_2_ = f32[4,40,128]{2,1,0:T(8,128)S(1)} collective-permute-done((f32[4,40,128]{2,1,0:T(8,128)S(1)}, f32[4,40,128]{2,1,0:T(8,128)S(1)}, u32[]{:S(2)}, u32[]{:S(2)}) %collective-permute-start.1) | collective-permute-done | bytes 81952 | tf_op jit(solution)/shard_map/ppermute | solution.py:325
  15.6 1.9 %collective-permute-start.2 = (f32[2,40,128]{2,1,0:T(8,128)S(1)}, f32[2,40,128]{2,1,0:T(8,128)S(1)}, u32[]{:S(2)}, u32[]{:S(2)}) collective-permute-start(f32[2,40,128]{2,1,0:T(8,128)S(1)} %get-tuple-element.21), channel_id=1, source_target_pairs={{0,2},{1,3},{2,0},{3,1},{4,6},{5,7},{6,4},{7,5},{8,10},{9,11},{10,... | collective-permute-start | bytes 122888 | tf_op jit(solution)/shard_map/ppermute | solution.py:325
  17.6 1.5 %collective-permute-start.3 = (f32[2,40,128]{2,1,0:T(8,128)S(1)}, f32[2,40,128]{2,1,0:T(8,128)S(1)}, u32[]{:S(2)}, u32[]{:S(2)}) collective-permute-start(f32[2,40,128]{2,1,0:T(8,128)S(1)} %get-tuple-element.20.refs_1_), channel_id=1, source_target_pairs={{0,16},{1,17},{2,18},{3,19},{4,20},{5,21},{6,22},{7,23},{8,24},{9,... | collective-permute-start | bytes 122888 | tf_op jit(solution)/shard_map/ppermute | solution.py:325
  19.1 0.1 collective-permute-start.4
  19.2 1.9 %collective-permute-done.2.refs_2_ = f32[2,40,128]{2,1,0:T(8,128)S(1)} collective-permute-done((f32[2,40,128]{2,1,0:T(8,128)S(1)}, f32[2,40,128]{2,1,0:T(8,128)S(1)}, u32[]{:S(2)}, u32[]{:S(2)}) %collective-permute-start.2) | collective-permute-done | bytes 40992 | tf_op jit(solution)/shard_map/ppermute | solution.py:325
  21.1 0.5 %collective-permute-done.3.refs_3_ = f32[2,40,128]{2,1,0:T(8,128)S(1)} collective-permute-done((f32[2,40,128]{2,1,0:T(8,128)S(1)}, f32[2,40,128]{2,1,0:T(8,128)S(1)}, u32[]{:S(2)}, u32[]{:S(2)}) %collective-permute-start.3) | collective-permute-done | bytes 40992 | tf_op jit(solution)/shard_map/ppermute | solution.py:325
  21.6 2.5 %collective-permute-done.4.refs_4_ = f32[2,40,128]{2,1,0:T(8,128)S(1)} collective-permute-done((f32[2,40,128]{2,1,0:T(8,128)S(1)}, f32[2,40,128]{2,1,0:T(8,128)S(1)}, u32[]{:S(2)}, u32[]{:S(2)}) %collective-permute-start.4) | collective-permute-done | bytes 40992 | tf_op jit(solution)/shard_map/ppermute | solution.py:325
  24.1 0.0 copy-start.3
  24.1 2.3 %collective-permute-start.5 = (f32[1,40,128]{2,1,0:T(8,128)S(1)}, f32[1,40,128]{2,1,0:T(8,128)S(1)}, u32[]{:S(2)}, u32[]{:S(2)}) collective-permute-start(f32[1,40,128]{2,1,0:T(8,128)S(1)} %get-tuple-element.23), channel_id=1, source_target_pairs={{0,4},{1,5},{2,6},{3,7},{4,0},{5,1},{6,2},{7,3},{8,12},{9,13},{10,... | collective-permute-start | bytes 61448 | tf_op jit(solution)/shard_map/ppermute | solution.py:325
  26.4 1.8 %collective-permute-done.5.refs_3_ = f32[1,40,128]{2,1,0:T(8,128)S(1)} collective-permute-done((f32[1,40,128]{2,1,0:T(8,128)S(1)}, f32[1,40,128]{2,1,0:T(8,128)S(1)}, u32[]{:S(2)}, u32[]{:S(2)}) %collective-permute-start.5) | collective-permute-done | bytes 20512 | tf_op jit(solution)/shard_map/ppermute | solution.py:325
  28.1 3.9 %all-to-all-done.refs_0_ = bf16[16,200,128]{2,1,0:T(8,128)(2,1)S(1)} async-done(((bf16[16,200,128]{2,1,0:T(8,128)(2,1)}), bf16[16,200,128]{2,1,0:T(8,128)(2,1)S(1)}, u32[]{:S(2)}, u32[]{:S(2)}) %all-to-all-start) | async-done | bytes 819232 | tf_op jit(solution)/shard_map/all_to_all | solution.py:329
  32.1 0.0 copy-done.3
  32.1 1.7 %receive.1 = (bf16[16,192,128]{2,1,0:T(8,128)(2,1)}, f32[16,24]{1,0:T(8,128)}, f32[16,256]{1,0:T(8,128)}) custom-call(bf16[16,200,128]{2,1,0:T(8,128)(2,1)S(1)} %all-to-all-done.refs_0_, s32[1,16]{1,0:T(1,128)S(1)} %copy-done.3, f32[1,40,128]{2,1,0:T(8,128)S(1)} %get-tuple-element.22.refs_2_, f32[1,40,128]{2,1,0:T(8,128)S(1)} %collective-permute-done.5.refs_3_), custom_call_target="tpu_custom_call" | custom-call | tf_op jit(solution)/shard_map/receive/pallas_call | solution.py:280
  (3 shorter events, 0.1 us)
Async XLA Ops:
  4.6 9.6 %collective-permute-start = (bf16[8,40,128]{2,1,0:T(8,128)(2,1)}, bf16[8,40,128]{2,1,0:T(8,128)(2,1)S(1)}, u32[]{:S(2)}, u32[]{:S(2)}) collective-permute-start(bf16[8,40,128]{2,1,0:T(8,128)(2,1)} %get-tuple-element.17), channel_id=1, source_target_pairs={{0,8},{1,9},{2,10},{3,11},{4,12},{5,13},{6,14},{7,15},{8,0},{9,1},... | collective-permute-start | bytes 245768 | tf_op jit(solution)/shard_map/ppermute | solution.py:325
  8.7 4.0 %copy-start = (bf16[8,256,192]{1,2,0:T(8,128)(2,1)S(1)}, bf16[8,256,192]{1,2,0:T(8,128)(2,1)}, u32[]{:S(2)}) copy-start(bf16[8,256,192]{1,2,0:T(8,128)(2,1)} %param.7) | copy-start | bytes 2359300
  8.7 4.0 %copy-start.1 = (bf16[8,256,192]{1,2,0:T(8,128)(2,1)S(1)}, bf16[8,256,192]{1,2,0:T(8,128)(2,1)}, u32[]{:S(2)}) copy-start(bf16[8,256,192]{1,2,0:T(8,128)(2,1)} %param.9) | copy-start | bytes 2359300
  8.7 23.4 %all-to-all-start = ((bf16[16,200,128]{2,1,0:T(8,128)(2,1)}), bf16[16,200,128]{2,1,0:T(8,128)(2,1)S(1)}, u32[]{:S(2)}, u32[]{:S(2)}) async-start(bf16[16,200,128]{2,1,0:T(8,128)(2,1)} %get-tuple-element.15), calls=%async_computation | async-start | bytes 1638400 | tf_op jit(solution)/shard_map/all_to_all | solution.py:329
  12.7 1.0 %copy-start.2 = (bf16[1536,128]{1,0:T(8,128)(2,1)S(1)}, bf16[1536,128]{1,0:T(8,128)(2,1)}, u32[]{:S(2)}) copy-start(bf16[1536,128]{1,0:T(8,128)(2,1)} %get-tuple-element.16.refs_3_) | copy-start | bytes 1179652
  14.2 1.4 %collective-permute-start.1 = (f32[4,40,128]{2,1,0:T(8,128)S(1)}, f32[4,40,128]{2,1,0:T(8,128)S(1)}, u32[]{:S(2)}, u32[]{:S(2)}) collective-permute-start(f32[4,40,128]{2,1,0:T(8,128)S(1)} %get-tuple-element.19), channel_id=1, source_target_pairs={{0,1},{1,0},{2,3},{3,2},{4,5},{5,4},{6,7},{7,6},{8,9},{9,8},{10,11... | collective-permute-start | bytes 245768 | tf_op jit(solution)/shard_map/ppermute | solution.py:325
  15.6 5.4 %collective-permute-start.2 = (f32[2,40,128]{2,1,0:T(8,128)S(1)}, f32[2,40,128]{2,1,0:T(8,128)S(1)}, u32[]{:S(2)}, u32[]{:S(2)}) collective-permute-start(f32[2,40,128]{2,1,0:T(8,128)S(1)} %get-tuple-element.21), channel_id=1, source_target_pairs={{0,2},{1,3},{2,0},{3,1},{4,6},{5,7},{6,4},{7,5},{8,10},{9,11},{10,... | collective-permute-start | bytes 122888 | tf_op jit(solution)/shard_map/ppermute | solution.py:325
  17.6 4.0 %collective-permute-start.3 = (f32[2,40,128]{2,1,0:T(8,128)S(1)}, f32[2,40,128]{2,1,0:T(8,128)S(1)}, u32[]{:S(2)}, u32[]{:S(2)}) collective-permute-start(f32[2,40,128]{2,1,0:T(8,128)S(1)} %get-tuple-element.20.refs_1_), channel_id=1, source_target_pairs={{0,16},{1,17},{2,18},{3,19},{4,20},{5,21},{6,22},{7,23},{8,24},{9,... | collective-permute-start | bytes 122888 | tf_op jit(solution)/shard_map/ppermute | solution.py:325
  19.1 5.0 %collective-permute-start.4 = (f32[2,40,128]{2,1,0:T(8,128)S(1)}, f32[2,40,128]{2,1,0:T(8,128)S(1)}, u32[]{:S(2)}, u32[]{:S(2)}) collective-permute-start(f32[2,40,128]{2,1,0:T(8,128)S(1)} %get-tuple-element.21), channel_id=1, source_target_pairs={{0,18},{1,19},{2,16},{3,17},{4,22},{5,23},{6,20},{7,21},{8,26},{9,... | collective-permute-start | bytes 122888 | tf_op jit(solution)/shard_map/ppermute | solution.py:325
  24.1 8.0 %copy-start.3 = (s32[1,16]{1,0:T(1,128)S(1)}, s32[1,16]{1,0:T(1,128)}, u32[]{:S(2)}) copy-start(s32[1,16]{1,0:T(1,128)} %refs_1_.1) | copy-start | bytes 196
  24.1 4.0 %collective-permute-start.5 = (f32[1,40,128]{2,1,0:T(8,128)S(1)}, f32[1,40,128]{2,1,0:T(8,128)S(1)}, u32[]{:S(2)}, u32[]{:S(2)}) collective-permute-start(f32[1,40,128]{2,1,0:T(8,128)S(1)} %get-tuple-element.23), channel_id=1, source_target_pairs={{0,4},{1,5},{2,6},{3,7},{4,0},{5,1},{6,2},{7,3},{8,12},{9,13},{10,... | collective-permute-start | bytes 61448 | tf_op jit(solution)/shard_map/ppermute | solution.py:325

commit v7 on v5

--- a/solution.py
+++ b/solution.py
@@ -131,7 +131,8 @@
             upper = rest[t * rows:t * rows + rows // 2, :]
             lower = rest[t * rows + rows // 2:(t + 1) * rows, :]
             out_ref[t, rows:rows + rows // 2, :] = jnp.where(left, upper, lower).astype(BF16)
-            out_ref[t, rows + rows // 2:, :] = gather_lanes(sources, t, local).astype(BF16)
+            mixed = gather_lanes(sources, t, local)
+            out_ref[t, rows + rows // 2:, :] = jnp.concatenate([mixed, mixed], axis=0).astype(BF16)
             sends[t].start()
     for copy in part_copies + sends:
         copy.wait()
@@ -164,7 +165,11 @@
     def weight_block(t):
         mine = comp_grad[t * comp_rows:(t + 1) * comp_rows]
         pieces = [mine[:, i * LANES:(i + 1) * LANES] for i in range(width // LANES)]
-        return jnp.concatenate(pieces + [gather_lanes(sources, t, local)], axis=0)
+        pieces.append(gather_lanes(sources, t, local))
+        used = comp_rows * (width // LANES) + 8
+        if used % 16:
+            pieces.append(jnp.zeros((16 - used % 16, LANES), F32))
+        return jnp.concatenate(pieces, axis=0)
 
     return [weight_block(t) for t in range(tables)]
 
@@ -263,7 +268,7 @@
     comp_width = comp.shape[0]
     comp_rows = comp_width // tables
     rows = local * count
-    total_rows = rows + rows // 2 + 8
+    total_rows = rows + rows // 2 + 16
     vmem = pl.BlockSpec(memory_space=pltpu.VMEM)
     smem = pl.BlockSpec(memory_space=pltpu.SMEM)
     hbm = pl.BlockSpec(memory_space=pltpu.HBM)
@@ -283,7 +288,7 @@
 
     x, h = jnp.swapaxes(emb, 1, 2), jnp.swapaxes(grad_comp, 1, 2)
     index = lax.axis_index("table").astype(jnp.int32).reshape(1)
-    part = comp_rows * (width // LANES) + 8
+    part = round_up(comp_rows * (width // LANES) + 8, 16)
     shapes = [
         ((tables, total_rows, LANES), BF16), ((tables // 2, part, LANES), F32), ((tables // 2, part, LANES), BF16)
     ]

time: 34.2 us -> 34.8 us (1.018)
  waiting for transfers between devices: 13.7 us -> 16 us
  starting transfers between devices: 13.7 us -> 12 us
    ppermute x6, waiting for transfers between devices: 9.25 us -> 11.7 us  [swap(): return lax.ppermute(array, ('dp', 'table'), pairs)]
    ppermute x6, starting transfers between devices: 9.7 us -> 7.95 us  [swap(): return lax.ppermute(array, ('dp', 'table'), pairs)]
where the time goes in v7:
time: 34.8 us; the launch traced here: 34.4 us
  waiting for transfers between devices  16 us (46%)
  starting transfers between devices  12 us (34%)
  Pallas kernels  5.78 us (17%)
  between operations  0.69 us (2%)
    ppermute x6, waiting for transfers between devices, swap(): return lax.ppermute(array, ('dp', 'table'), pairs)  11.7 us
    ppermute x6, starting transfers between devices, swap(): return lax.ppermute(array, ('dp', 'table'), pairs)  7.95 us
    pallas_call x5, Pallas kernels, call(): pl.pallas_call(body, out_shape=tuple((jax.ShapeDtypeStruct(*o) for o in o...  5.78 us
    all_to_all x1, waiting for transfers between devices, shards(): got = lax.all_to_all(sent, 'table', split_axis=0, concat_axis=0, tiled=True)  4.31 us
    all_to_all x1, starting transfers between devices, shards(): got = lax.all_to_all(sent, 'table', split_axis=0, concat_axis=0, tiled=True)  4.01 us
  transfers between devices with their start and end apart: 7, of which 6 were waited for; matrix products, arithmetic and copies ran while one was open for 0% of the time, Pallas kernels for 0%

profile of v7, /device:TPU:0, one launch (start us, length us, event | category | flops | bytes accessed | tf_op | source)
XLA Modules:
  0.0 34.4 jit_solution(5425681874747922541)
XLA Ops:
  0.6 4.1 %send.1 = (bf16[16,208,128]{2,1,0:T(8,128)(2,1)}, f32[8,48,128]{2,1,0:T(8,128)}, bf16[8,48,128]{2,1,0:T(8,128)(2,1)}) custom-call(s32[1]{0:T(128)} %bitcast.refs_0_, bf16[8,192,256]{2,1,0:T(8,128)(2,1)} %bitcast.7, bf16[8,192,256]{2,1,0:T(8,128)(2,1)} %bitcast.8, bf16[8,6144]{1,0:T(8,128)(2,1)} %refs_3_.1, bf16[24,256]{1,0:T(8,128)(2,1)} %bitcast.9, ...), custom_call_target="tpu_custom_call" | custom-call | tf_op jit(solution)/shard_map/send/pallas_call | solution.py:279
  4.7 4.1 %collective-permute-start = (bf16[8,48,128]{2,1,0:T(8,128)(2,1)}, bf16[8,48,128]{2,1,0:T(8,128)(2,1)S(1)}, u32[]{:S(2)}, u32[]{:S(2)}) collective-permute-start(bf16[8,48,128]{2,1,0:T(8,128)(2,1)} %get-tuple-element.17), channel_id=1, source_target_pairs={{0,8},{1,9},{2,10},{3,11},{4,12},{5,13},{6,14},{7,15},{8,0},{9,1},... | collective-permute-start | bytes 294920 | tf_op jit(solution)/shard_map/ppermute | solution.py:324
  8.8 0.0 copy-start.1
  8.8 4.0 %all-to-all-start = ((bf16[16,208,128]{2,1,0:T(8,128)(2,1)}), bf16[16,208,128]{2,1,0:T(8,128)(2,1)S(1)}, u32[]{:S(2)}, u32[]{:S(2)}) async-start(bf16[16,208,128]{2,1,0:T(8,128)(2,1)} %get-tuple-element.15), calls=%async_computation | async-start | bytes 1703936 | tf_op jit(solution)/shard_map/all_to_all | solution.py:328
  12.9 1.1 %collective-permute-done.refs_2_ = bf16[8,48,128]{2,1,0:T(8,128)(2,1)S(1)} collective-permute-done((bf16[8,48,128]{2,1,0:T(8,128)(2,1)}, bf16[8,48,128]{2,1,0:T(8,128)(2,1)S(1)}, u32[]{:S(2)}, u32[]{:S(2)}) %collective-permute-start) | collective-permute-done | bytes 98336 | tf_op jit(solution)/shard_map/ppermute | solution.py:324
  13.9 0.0 copy-done.1
  14.0 0.1 collective-permute-start.1
  14.0 1.3 %collective-permute-done.1.refs_2_ = f32[4,48,128]{2,1,0:T(8,128)S(1)} collective-permute-done((f32[4,48,128]{2,1,0:T(8,128)S(1)}, f32[4,48,128]{2,1,0:T(8,128)S(1)}, u32[]{:S(2)}, u32[]{:S(2)}) %collective-permute-start.1) | collective-permute-done | bytes 98336 | tf_op jit(solution)/shard_map/ppermute | solution.py:324
  15.4 1.6 %collective-permute-start.2 = (f32[2,48,128]{2,1,0:T(8,128)S(1)}, f32[2,48,128]{2,1,0:T(8,128)S(1)}, u32[]{:S(2)}, u32[]{:S(2)}) collective-permute-start(f32[2,48,128]{2,1,0:T(8,128)S(1)} %get-tuple-element.21), channel_id=1, source_target_pairs={{0,2},{1,3},{2,0},{3,1},{4,6},{5,7},{6,4},{7,5},{8,10},{9,11},{10,... | collective-permute-start | bytes 147464 | tf_op jit(solution)/shard_map/ppermute | solution.py:324
  17.0 1.5 %collective-permute-start.3 = (f32[2,48,128]{2,1,0:T(8,128)S(1)}, f32[2,48,128]{2,1,0:T(8,128)S(1)}, u32[]{:S(2)}, u32[]{:S(2)}) collective-permute-start(f32[2,48,128]{2,1,0:T(8,128)S(1)} %get-tuple-element.20.refs_1_), channel_id=1, source_target_pairs={{0,16},{1,17},{2,18},{3,19},{4,20},{5,21},{6,22},{7,23},{8,24},{9,... | collective-permute-start | bytes 147464 | tf_op jit(solution)/shard_map/ppermute | solution.py:324
  18.5 0.4 %collective-permute-start.4 = (f32[2,48,128]{2,1,0:T(8,128)S(1)}, f32[2,48,128]{2,1,0:T(8,128)S(1)}, u32[]{:S(2)}, u32[]{:S(2)}) collective-permute-start(f32[2,48,128]{2,1,0:T(8,128)S(1)} %get-tuple-element.21), channel_id=1, source_target_pairs={{0,18},{1,19},{2,16},{3,17},{4,22},{5,23},{6,20},{7,21},{8,26},{9,... | collective-permute-start | bytes 147464 | tf_op jit(solution)/shard_map/ppermute | solution.py:324
  18.9 4.0 %collective-permute-done.2.refs_2_ = f32[2,48,128]{2,1,0:T(8,128)S(1)} collective-permute-done((f32[2,48,128]{2,1,0:T(8,128)S(1)}, f32[2,48,128]{2,1,0:T(8,128)S(1)}, u32[]{:S(2)}, u32[]{:S(2)}) %collective-permute-start.2) | collective-permute-done | bytes 49184 | tf_op jit(solution)/shard_map/ppermute | solution.py:324
  22.9 0.0 collective-permute-done.3.refs_3_
  22.9 1.7 %collective-permute-done.4.refs_4_ = f32[2,48,128]{2,1,0:T(8,128)S(1)} collective-permute-done((f32[2,48,128]{2,1,0:T(8,128)S(1)}, f32[2,48,128]{2,1,0:T(8,128)S(1)}, u32[]{:S(2)}, u32[]{:S(2)}) %collective-permute-start.4) | collective-permute-done | bytes 49184 | tf_op jit(solution)/shard_map/ppermute | solution.py:324
  24.6 0.0 copy-start
  24.6 0.2 collective-permute-start.5
  24.8 3.7 %collective-permute-done.5.refs_3_ = f32[1,48,128]{2,1,0:T(8,128)S(1)} collective-permute-done((f32[1,48,128]{2,1,0:T(8,128)S(1)}, f32[1,48,128]{2,1,0:T(8,128)S(1)}, u32[]{:S(2)}, u32[]{:S(2)}) %collective-permute-start.5) | collective-permute-done | bytes 24608 | tf_op jit(solution)/shard_map/ppermute | solution.py:324
  28.5 4.3 %all-to-all-done.refs_0_ = bf16[16,208,128]{2,1,0:T(8,128)(2,1)S(1)} async-done(((bf16[16,208,128]{2,1,0:T(8,128)(2,1)}), bf16[16,208,128]{2,1,0:T(8,128)(2,1)S(1)}, u32[]{:S(2)}, u32[]{:S(2)}) %all-to-all-start) | async-done | bytes 852000 | tf_op jit(solution)/shard_map/all_to_all | solution.py:328
  32.8 0.0 copy-done
  32.8 1.7 %receive.1 = (bf16[16,192,128]{2,1,0:T(8,128)(2,1)}, f32[16,24]{1,0:T(8,128)}, f32[16,256]{1,0:T(8,128)}) custom-call(bf16[16,208,128]{2,1,0:T(8,128)(2,1)S(1)} %all-to-all-done.refs_0_, s32[1,16]{1,0:T(1,128)S(1)} %copy-done, f32[1,48,128]{2,1,0:T(8,128)S(1)} %get-tuple-element.22.refs_2_, f32[1,48,128]{2,1,0:T(8,128)S(1)} %collective-permute-done.5.refs_3_), custom_call_target="tpu_custom_call" | custom-call | tf_op jit(solution)/shard_map/receive/pallas_call | solution.py:279
  (3 shorter events, 0.1 us)
Async XLA Ops:
  4.7 9.2 %collective-permute-start = (bf16[8,48,128]{2,1,0:T(8,128)(2,1)}, bf16[8,48,128]{2,1,0:T(8,128)(2,1)S(1)}, u32[]{:S(2)}, u32[]{:S(2)}) collective-permute-start(bf16[8,48,128]{2,1,0:T(8,128)(2,1)} %get-tuple-element.17), channel_id=1, source_target_pairs={{0,8},{1,9},{2,10},{3,11},{4,12},{5,13},{6,14},{7,15},{8,0},{9,1},... | collective-permute-start | bytes 294920 | tf_op jit(solution)/shard_map/ppermute | solution.py:324
  8.8 5.1 %copy-start.1 = (f32[8,48,128]{2,1,0:T(8,128)S(1)}, f32[8,48,128]{2,1,0:T(8,128)}, u32[]{:S(2)}) copy-start(f32[8,48,128]{2,1,0:T(8,128)} %get-tuple-element.16.refs_1_) | copy-start | bytes 589828
  8.8 23.9 %all-to-all-start = ((bf16[16,208,128]{2,1,0:T(8,128)(2,1)}), bf16[16,208,128]{2,1,0:T(8,128)(2,1)S(1)}, u32[]{:S(2)}, u32[]{:S(2)}) async-start(bf16[16,208,128]{2,1,0:T(8,128)(2,1)} %get-tuple-element.15), calls=%async_computation | async-start | bytes 1703936 | tf_op jit(solution)/shard_map/all_to_all | solution.py:328
  14.0 1.4 %collective-permute-start.1 = (f32[4,48,128]{2,1,0:T(8,128)S(1)}, f32[4,48,128]{2,1,0:T(8,128)S(1)}, u32[]{:S(2)}, u32[]{:S(2)}) collective-permute-start(f32[4,48,128]{2,1,0:T(8,128)S(1)} %get-tuple-element.19), channel_id=1, source_target_pairs={{0,1},{1,0},{2,3},{3,2},{4,5},{5,4},{6,7},{7,6},{8,9},{9,8},{10,11... | collective-permute-start | bytes 294920 | tf_op jit(solution)/shard_map/ppermute | solution.py:324
  15.4 7.5 %collective-permute-start.2 = (f32[2,48,128]{2,1,0:T(8,128)S(1)}, f32[2,48,128]{2,1,0:T(8,128)S(1)}, u32[]{:S(2)}, u32[]{:S(2)}) collective-permute-start(f32[2,48,128]{2,1,0:T(8,128)S(1)} %get-tuple-element.21), channel_id=1, source_target_pairs={{0,2},{1,3},{2,0},{3,1},{4,6},{5,7},{6,4},{7,5},{8,10},{9,11},{10,... | collective-permute-start | bytes 147464 | tf_op jit(solution)/shard_map/ppermute | solution.py:324
  17.0 5.9 %collective-permute-start.3 = (f32[2,48,128]{2,1,0:T(8,128)S(1)}, f32[2,48,128]{2,1,0:T(8,128)S(1)}, u32[]{:S(2)}, u32[]{:S(2)}) collective-permute-start(f32[2,48,128]{2,1,0:T(8,128)S(1)} %get-tuple-element.20.refs_1_), channel_id=1, source_target_pairs={{0,16},{1,17},{2,18},{3,19},{4,20},{5,21},{6,22},{7,23},{8,24},{9,... | collective-permute-start | bytes 147464 | tf_op jit(solution)/shard_map/ppermute | solution.py:324
  18.5 6.1 %collective-permute-start.4 = (f32[2,48,128]{2,1,0:T(8,128)S(1)}, f32[2,48,128]{2,1,0:T(8,128)S(1)}, u32[]{:S(2)}, u32[]{:S(2)}) collective-permute-start(f32[2,48,128]{2,1,0:T(8,128)S(1)} %get-tuple-element.21), channel_id=1, source_target_pairs={{0,18},{1,19},{2,16},{3,17},{4,22},{5,23},{6,20},{7,21},{8,26},{9,... | collective-permute-start | bytes 147464 | tf_op jit(solution)/shard_map/ppermute | solution.py:324
  24.6 8.2 %copy-start = (s32[1,16]{1,0:T(1,128)S(1)}, s32[1,16]{1,0:T(1,128)}, u32[]{:S(2)}) copy-start(s32[1,16]{1,0:T(1,128)} %refs_1_.1) | copy-start | bytes 196
  24.6 3.9 %collective-permute-start.5 = (f32[1,48,128]{2,1,0:T(8,128)S(1)}, f32[1,48,128]{2,1,0:T(8,128)S(1)}, u32[]{:S(2)}, u32[]{:S(2)}) collective-permute-start(f32[1,48,128]{2,1,0:T(8,128)S(1)} %get-tuple-element.23), channel_id=1, source_target_pairs={{0,4},{1,5},{2,6},{3,7},{4,0},{5,1},{6,2},{7,3},{8,12},{9,13},{10,... | collective-permute-start | bytes 73736 | tf_op jit(solution)/shard_map/ppermute | solution.py:324
